TPU v7x, 32 devices: a whole 2x2x4 slice. The times are simulated.
32 devices in a mesh: row: 8 (over y, x, core), col: 4 (over z).
Axes of the slice: x: 2, y: 2, z: 4, core: 2. Of those that a mesh axis runs over, the one named last changes fastest.
Arguments:
- hidden_in: bfloat16 [2048, 7168], P('row'), may hold values from -6 to 6
- norm_gain: float32 [7168], replicated, may hold values from 0.5 to 1.5
- norm_bias: float32 [7168], replicated, may hold values from -3 to 3
- w_query: bfloat16 [7168, 6144], P('row', 'col'), may hold values from -0.0625 to 0.0625
- w_keyval: bfloat16 [7168, 2, 6144], P('row', None, 'col'), may hold values from -0.125 to 0.125
- bias_query: float32 [6144], P('col'), may hold values from -3 to 3
- bias_keyval: float32 [2, 6144], P(None, 'col'), may hold values from -3 to 3
- cache_keys: bfloat16 [8, 4096, 6144], P('row', None, 'col'), may hold values from -60 to 60
- cache_values: bfloat16 [8, 4096, 6144], P('row', None, 'col'), may hold values from -12 to 12
- cache_lengths: int32 [8], replicated, may hold values from 2 to 4096
- owner_slot: int32 [8], replicated, may hold values from 0 to 7, each once
- w_out: bfloat16 [6144, 7168], P('col', 'row'), may hold values from -0.3125 to 0.3125
- bias_out: float32 [7168], P('col'), may hold values from -3 to 3
Outputs:
- hidden_out: bfloat16 [2048, 7168], P('row', 'col')
- new_keys: bfloat16 [8, 256, 6144], P('row', None, 'col')
- new_values: bfloat16 [8, 256, 6144], P('row', None, 'col')
Inputs may be any that keep to these rules, and one draw needn't show every extreme that they name: `owner_slot`: each slot is the owner of exactly one request.
All inputs are finite; a program needn't handle non-finite values.
Results may differ from a plain program's by a relative error of at most 0.01375.
Values may be sent and summed in bfloat16 or wider, within the bound.
No kernel may reach another device: no remote copies, remote signals or barrier semaphores. Data moves between devices by JAX's collectives and lax.ppermute only.
A program may use at most 192 MiB of HBM per device.

v0:
```python
import jax
import jax.numpy as jnp
from jax import lax
from jax.sharding import PartitionSpec as P

HEAD = 128


def normalize(inputs, gain, bias):
    row_mean = jnp.mean(inputs, axis=-1, keepdims=True)
    centered = inputs - row_mean
    row_var = jnp.mean(centered * centered, axis=-1, keepdims=True)
    return centered * lax.rsqrt(row_var + 1e-05) * gain + bias


def visit_block(carried, key_block, value_block, is_valid, query_heads):
    row_max, row_sum, weighted = carried
    scores = jnp.einsum("qhd,khd->hqk", query_heads, key_block, preferred_element_type=jnp.float32)
    scores = jnp.where(is_valid[None], scores, -1e30)
    new_max = jnp.maximum(row_max, jnp.max(scores, axis=-1))
    probs = jnp.where(is_valid[None], jnp.exp(scores - new_max[..., None]), 0.0)
    factor = jnp.exp(row_max - new_max)
    row_sum = row_sum * factor + jnp.sum(probs, axis=-1)
    weighted = weighted * factor[..., None] + jnp.einsum(
        "hqk,khd->hqd", probs.astype(jnp.bfloat16), value_block, preferred_element_type=jnp.float32
    )
    return (new_max, row_sum, weighted)


def local(
    hidden_in,
    norm_gain,
    norm_bias,
    w_query,
    w_keyval,
    bias_query,
    bias_keyval,
    cache_keys,
    cache_values,
    cache_lengths,
    owner_slot,
    w_out,
    bias_out,
):
    row_id = lax.axis_index("row")
    col_id = lax.axis_index("col")
    group_len = hidden_in.shape[0]
    head_cols = w_query.shape[1]
    head_count = head_cols // HEAD
    req_count = owner_slot.shape[0]
    q_scale = HEAD ** (-0.5)
    slot_ids = jnp.arange(req_count, dtype=jnp.int32)
    is_owner = owner_slot[:, None] == slot_ids[None, :]
    inverse = jnp.sum(jnp.where(is_owner, slot_ids[:, None], 0), axis=0)
    my_request = inverse[row_id]
    my_slot = owner_slot[row_id]
    inputs = hidden_in.astype(jnp.float32)
    normed = normalize(inputs, norm_gain, norm_bias).astype(jnp.bfloat16)
    bias_kv_flat = bias_keyval.reshape(2 * head_cols)
    pieces = (
        lax.all_gather(w_query, "row", axis=0, tiled=True),
        lax.all_gather(w_keyval, "row", axis=0, tiled=True),
    )
    query_part = jnp.dot(normed, pieces[0], preferred_element_type=jnp.float32)
    kv_part = jnp.dot(
        normed,
        pieces[1].reshape(pieces[1].shape[0], 2 * head_cols),
        preferred_element_type=jnp.float32,
    )
    own_query = ((query_part + bias_query) * q_scale).astype(jnp.bfloat16)
    own_kv = (kv_part + bias_kv_flat).astype(jnp.bfloat16)
    every_query, every_kv = (
        lax.all_gather(own_query, "row", axis=0, tiled=True),
        lax.all_gather(own_kv, "row", axis=0, tiled=True),
    )
    query_rows = lax.dynamic_slice_in_dim(every_query, my_request * group_len, group_len, 0)
    keyval = lax.dynamic_slice_in_dim(every_kv, my_request * group_len, group_len, 0)
    new_k = keyval[:, :head_cols]
    new_v = keyval[:, head_cols:]
    query_heads = query_rows.reshape(group_len, head_count, HEAD)
    cache_len = cache_keys.shape[1]
    key_len = min(512, cache_len)
    all_blocks = cache_len // key_len
    cache_k = cache_keys[0].reshape(cache_len, head_count, HEAD)
    cache_v = cache_values[0].reshape(cache_len, head_count, HEAD)
    length = cache_lengths[my_request]

    def cache_step(index, carried):
        key_block = lax.dynamic_slice_in_dim(cache_k, index * key_len, key_len, 0)
        value_block = lax.dynamic_slice_in_dim(cache_v, index * key_len, key_len, 0)
        positions = index * key_len + jnp.arange(key_len, dtype=jnp.int32)
        is_valid = (positions < length)[None, :]
        return visit_block(carried, key_block, value_block, is_valid, query_heads)

    start_max = jnp.full((head_count, group_len), -1e30, jnp.float32)
    start_sum = jnp.zeros((head_count, group_len), jnp.float32)
    start_weighted = jnp.zeros((head_count, group_len, HEAD), jnp.float32)
    carried = lax.fori_loop(0, all_blocks, cache_step, (start_max, start_sum, start_weighted))
    group_pos = jnp.arange(group_len, dtype=jnp.int32)
    causal = group_pos[:, None] >= group_pos[None, :]
    carried = visit_block(
        carried,
        new_k.reshape(group_len, head_count, HEAD),
        new_v.reshape(group_len, head_count, HEAD),
        causal,
        query_heads,
    )
    attended = (
        (carried[2] / carried[1][..., None])
        .transpose(1, 0, 2)
        .reshape(group_len, head_cols)
        .astype(jnp.bfloat16)
    )
    gathered = lax.all_gather(attended, "row", axis=0, tiled=True)
    my_rows = lax.dynamic_slice_in_dim(gathered, my_slot * group_len, group_len, 0)
    partial_value = jnp.dot(
        my_rows,
        lax.all_gather(w_out, "row", axis=1, tiled=True),
        preferred_element_type=jnp.float32,
    )
    summed_out = lax.psum_scatter(
        partial_value.astype(jnp.bfloat16), "col", scatter_dimension=1, tiled=True
    ).astype(jnp.float32)
    out_cols = summed_out.shape[1]
    residual = lax.dynamic_slice_in_dim(inputs, col_id * out_cols, out_cols, 1)
    hidden_out = (summed_out + bias_out + residual).astype(jnp.bfloat16)
    return (
        hidden_out,
        new_k.reshape(1, group_len, head_cols),
        new_v.reshape(1, group_len, head_cols),
    )


def solution(mesh):
    placed = (
        P("row", None),
        P(),
        P(),
        P("row", "col"),
        P("row", None, "col"),
        P("col"),
        P(None, "col"),
        P("row", None, "col"),
        P("row", None, "col"),
        P(),
        P(),
        P("col", "row"),
        P("col"),
    )
    return jax.shard_map(
        local,
        mesh=mesh,
        in_specs=placed,
        out_specs=(P("row", "col"), P("row", None, "col"), P("row", None, "col")),
        check_vma=False,
    )
```

profile of v0, /device:TPU:0, one launch (start us, length us, event | category | flops | bytes accessed | tf_op | source)
XLA Modules:
  0.0 736.6 jit_solution(14259600512634103882)
XLA Ops:
  13.0 111.7 %all-gather.7.cloned.1.call-done = bf16[7168,1536]{1,0:T(8,128)(2,1)} async-done(((bf16[896,1536]{1,0:T(8,128)(2,1)}), bf16[7168,1536]{1,0:T(8,128)(2,1)}) %all-gather.7.cloned.1.call-update) | async-done | bytes 22020112 | tf_op jit(solution)/shard_map/all_gather | solution.py:61
  124.7 12.8 %fusion.26 = bf16[256,1536]{1,0:T(8,128)(2,1)} fusion(bf16[7168,1536]{1,0:T(8,128)(2,1)} %all-gather.7.cloned.1.call-done, f32[1536]{0:T(1024)S(1)} %copy-done.11, bf16[256,7168]{1,0:T(8,128)(2,1)} %param.15, f32[7168]{0:T(1024)S(1)} %copy-done.9, f32[7168]{0:T(1024)S(1)} %copy-done.10, f32[256]{0:T(256)S(1)} %add_rsqrt_fusion, ...), kind=kOutput, calls=%fused_computation.36 | convolution fusion | flops 5649334272 | bytes 26542080 | tf_op jit(solution)/shard_map/dot_general | solution.py:64
  137.6 194.9 %all-gather.11.cloned.1.call-done = bf16[7168,2,1536]{2,1,0:T(2,128)(2,1)} async-done(((bf16[896,2,1536]{2,1,0:T(2,128)(2,1)}), bf16[7168,2,1536]{2,1,0:T(2,128)(2,1)}) %all-gather.11.cloned.1.call-update) | async-done | bytes 44040208 | tf_op jit(solution)/shard_map/all_gather | solution.py:62
  332.5 29.8 %copy.66 = bf16[896,8,2,1536]{3,1,2,0:T(8,128)(2,1)} copy(bf16[896,8,2,1536]{3,2,1,0:T(2,128)(2,1)} %bitcast.44) | data formatting | bytes 88080384
  362.3 21.8 %fusion.24 = bf16[256,3072]{1,0:T(8,128)(2,1)} fusion(bf16[7168,3072]{1,0:T(8,128)(2,1)} %bitcast.45, f32[3072]{0:T(1024)S(1)} %add.136, bf16[256,7168]{1,0:T(8,128)(2,1)} %param.15, f32[7168]{0:T(1024)S(1)} %copy-done.9, f32[7168]{0:T(1024)S(1)} %copy-done.10, f32[256]{0:T(256)S(1)} %add_rsqrt_fusion, f32[256]{0:T(256)S(1)} %broadcast_multiply_fusion), kind=kOutput, calls=%fused_computation.31 | convolution fusion | flops 11286872064 | bytes 49354752 | tf_op jit(solution)/shard_map/dot_general | solution.py:65
  387.6 16.1 %copy.48 = bf16[1,4096,1536]{1,2,0:T(8,128)(2,1)} copy(bf16[1,4096,1536]{2,1,0:T(8,128)(2,1)} %param.22) | data formatting | bytes 25165824 | tf_op args[7]
  403.7 16.1 %copy.50 = bf16[1,4096,1536]{1,2,0:T(8,128)(2,1)} copy(bf16[1,4096,1536]{2,1,0:T(8,128)(2,1)} %param.23) | data formatting | bytes 25165824 | tf_op args[8]
  421.2 34.9 %all-gather.13.cloned.1.call-done = bf16[2048,3072]{1,0:T(8,128)(2,1)} async-done(((bf16[256,3072]{1,0:T(8,128)(2,1)}), bf16[2048,3072]{1,0:T(8,128)(2,1)}) %all-gather.13.cloned.1.call-update) | async-done | bytes 12582928 | tf_op jit(solution)/shard_map/all_gather | solution.py:74
  459.8 128.8 %while.18 = (s32[]{:T(128)}, f32[12,256]{1,0:T(8,128)S(1)}, f32[12,256]{1,0:T(8,128)S(1)}, f32[12,256,128]{2,1,0:T(8,128)}, s32[]{:T(128)}, /*index=5*/bf16[4096...) while((s32[]{:T(128)}, f32[12,256]{1,0:T(8,128)S(1)}, ...), condition=%wide.region_6.7_spmd.clone, body=%wide.region_3.6_spmd.clone.sunk | while | flops 822231040 | bytes 51325656 | solution.py:98
  460.4 6.1 bitcast_reduce_fusion.2
  478.0 5.3 bitcast_reduce_fusion.2
  493.8 5.3 bitcast_reduce_fusion.2
  503.7 5.2 fusion.59
  509.6 5.3 bitcast_reduce_fusion.2
  519.6 5.2 fusion.59
  525.5 5.6 bitcast_reduce_fusion.2
  541.7 5.3 bitcast_reduce_fusion.2
  557.5 5.3 bitcast_reduce_fusion.2
  567.5 5.4 fusion.59
  573.5 5.3 bitcast_reduce_fusion.2
  597.8 45.5 %all-gather.15.cloned.1.call-done = bf16[2048,1536]{0,1:T(8,128)(2,1)} async-done(((bf16[256,1536]{0,1:T(8,128)(2,1)}), bf16[2048,1536]{0,1:T(8,128)(2,1)}) %all-gather.15.cloned.1.call-update) | async-done | bytes 6291472 | tf_op jit(solution)/shard_map/all_gather | solution.py:114
  643.3 15.0 %convolution_convert_fusion = bf16[256,7168]{1,0:T(8,128)(2,1)} fusion(bf16[1536,7168]{1,0:T(8,128)(2,1)} %all-gather.17.cloned.1.call-done, bf16[2048,1536]{0,1:T(8,128)(2,1)} %all-gather.15.cloned.1.call-done, s32[]{:T(128)S(6)} %select_n.60), kind=kOutput, calls=%fused_computation.26 | convolution fusion | flops 5638979584 | bytes 26476548 | tf_op jit(solution)/shard_map/dot_general | solution.py:116
  658.3 5.9 convert_element_type.40
  664.2 62.7 %reduce-scatter.2.cloned.1.call-done = bf16[256,1792]{1,0:T(8,128)(2,1)} async-done(((bf16[256,7168]{1,0:T(8,128)(2,1)}), bf16[256,1792]{1,0:T(8,128)(2,1)}) %reduce-scatter.2.cloned.1.call-update) | async-done | bytes 917520 | tf_op jit(solution)/shard_map/reduce_scatter | solution.py:121
  (128 shorter events, 92.5 us)
Async XLA Ops:
  7.2 117.5 %all-gather.7.cloned.1.call-start = ((), (), s32[]{:S(2)}) async-start(), calls=%async_computation.1 | async-start | bytes 24772608 | tf_op jit(solution)/shard_map/all_gather | solution.py:61
  7.9 324.6 %all-gather.11.cloned.1.call-start = ((), (), s32[]{:S(2)}) async-start(), calls=%async_computation.3 | async-start | bytes 49545216 | tf_op jit(solution)/shard_map/all_gather | solution.py:62
  8.6 412.6 %all-gather.9.cloned.1.call-start = ((), (), s32[]{:S(2)}) async-start(), calls=%async_computation.2 | async-start | bytes 7077888 | tf_op jit(solution)/shard_map/all_gather | solution.py:73
  8.7 3.1 copy-start.1
  8.7 115.9 %copy-start.9 = (f32[7168]{0:T(1024)S(1)}, f32[7168]{0:T(1024)}, u32[]{:S(2)}) copy-start(f32[7168]{0:T(1024)} %param.17) | copy-start | bytes 86020
  8.7 115.9 %copy-start.10 = (f32[7168]{0:T(1024)S(1)}, f32[7168]{0:T(1024)}, u32[]{:S(2)}) copy-start(f32[7168]{0:T(1024)} %param.16) | copy-start | bytes 86020
  8.7 115.9 %copy-start.11 = (f32[1536]{0:T(1024)S(1)}, f32[1536]{0:T(1024)}, u32[]{:S(2)}) copy-start(f32[1536]{0:T(1024)} %param.20) | copy-start | bytes 18436
  13.0 124.6 %copy-start.7 = (f32[2,1536]{1,0:T(2,128)S(1)}, f32[2,1536]{1,0:T(2,128)}, u32[]{:S(2)}) copy-start(f32[2,1536]{1,0:T(2,128)} %param.21) | copy-start | bytes 36868
  137.5 318.6 %all-gather.13.cloned.1.call-start = ((), (), s32[]{:S(2)}) async-start(), calls=%async_computation.4 | async-start | bytes 14155776 | tf_op jit(solution)/shard_map/all_gather | solution.py:74
  384.1 213.7 %all-gather.17.cloned.1.call-start = ((), (), s32[]{:S(2)}) async-start(), calls=%async_computation.6 | async-start | bytes 24772608 | tf_op jit(solution)/shard_map/all_gather | solution.py:118
  384.7 258.5 %all-gather.15.cloned.1.call-start = ((), (), s32[]{:S(2)}) async-start(), calls=%async_computation.5 | async-start | bytes 7077888 | tf_op jit(solution)/shard_map/all_gather | solution.py:114
  403.7 16.8 %copy-start.12 = (s32[8]{0:T(128)S(1)}, s32[8]{0:T(128)}, u32[]{:S(2)}) copy-start(s32[8]{0:T(128)} %param.24) | copy-start | bytes 100
  457.9 133.8 %copy-start.3 = (bf16[256,1536]{1,0:T(8,128)(2,1)}, bf16[256,1536]{1,0:T(8,128)(2,1)S(1)}, u32[]{:S(2)}) copy-start(bf16[256,1536]{1,0:T(8,128)(2,1)S(1)} %get-tuple-element.221) | copy-start | bytes 2359300
  466.5 6.1 copy-start
  483.3 4.6 copy-start
  499.1 4.6 copy-start
  514.8 4.8 copy-start
  531.1 4.8 copy-start
  547.0 4.6 copy-start
  562.8 4.7 copy-start
  578.8 4.6 copy-start
  588.6 4.3 copy-start.4
  596.3 130.6 %reduce-scatter.2.cloned.1.call-start = ((), (), s32[]{:S(2)}) async-start(), calls=%async_computation.7 | async-start | bytes 4587520 | tf_op jit(solution)/shard_map/reduce_scatter | solution.py:121
  658.3 68.6 %copy-start.8 = (f32[1792]{0:T(1024)S(1)}, f32[1792]{0:T(1024)}, u32[]{:S(2)}) copy-start(f32[1792]{0:T(1024)} %param.27) | copy-start | bytes 21508
  (4 other events, 5.7 us)
Sparse Core Ops, SparseCore 0:
  9.9 114.7 all-gather.6
  126.6 205.9 all-gather.10
  335.0 45.5 all-gather.8
  384.3 71.8 all-gather.12
  457.9 111.3 all-gather.16
  596.4 46.7 all-gather.14
  658.4 68.3 reduce-scatter.1
where the time goes:
time: 738 us; the launch traced here: 737 us
  waiting for transfers between devices  452 us (61%)
  matrix products  137 us (19%)
  local copies, waits for them, and re-layouts  80 us (11%)
  other arithmetic  49.7 us (7%)
  between operations  17.5 us (2%)
    all_gather x1, waiting for transfers between devices, local(): lax.all_gather(w_keyval, 'row', axis=0, tiled=True)  195 us
    all_gather x1, waiting for transfers between devices, local(): lax.all_gather(w_query, 'row', axis=0, tiled=True)  112 us
    unnamed x30, local copies, waits for them, and re-layouts  63 us
    reduce_scatter x1, waiting for transfers between devices, local(): lax.psum_scatter(partial_value.astype(jnp.bfloat16), 'col', scatter_dimen...  62.7 us
    all_gather x1, waiting for transfers between devices, local(): gathered = lax.all_gather(attended, 'row', axis=0, tiled=True)  45.5 us
    dot_general x9, matrix products, visit_block(): jnp.einsum('qhd,khd->hqk', query_heads, key_block, preferred_element_type...  44 us
    dot_general x9, matrix products, visit_block(): jnp.einsum('hqk,khd->hqd', probs.astype(jnp.bfloat16), value_block, prefe...  43.2 us
    all_gather x1, waiting for transfers between devices, local(): lax.all_gather(own_kv, 'row', axis=0, tiled=True)  34.9 us
  transfers between devices with their start and end apart: 7, of which 5 were waited for; matrix products, arithmetic and copies ran while one was open for 33% of the time, Pallas kernels for 0%

commit v1 on v0

v1 whole, which is shorter than its diff:
```python
import functools

import jax
import jax.numpy as jnp
from jax import lax
from jax.experimental import pallas as pl
from jax.experimental.pallas import tpu as pltpu
from jax.sharding import PartitionSpec as P

HEAD = 128
F32 = jnp.float32
BF16 = jnp.bfloat16


def normalize(inputs, gain, bias):
    row_mean = jnp.mean(inputs, axis=-1, keepdims=True)
    centered = inputs - row_mean
    row_var = jnp.mean(centered * centered, axis=-1, keepdims=True)
    return centered * lax.rsqrt(row_var + 1e-05) * gain + bias


def swap(value, axis, mask, size):
    return lax.ppermute(value, axis, [(i, i ^ mask) for i in range(size)])


def gather_block(table, places, dst, sem):
    for at, place in enumerate(places):

        @pl.when(table == at)
        def _(place=place):
            pltpu.make_async_copy(place, dst, sem).start()


def project_kernel(meta_ref, *refs, blocks, group, orders):
    x_refs, (wq_ref, wkv_ref, taken_ref) = refs[:blocks], refs[blocks : blocks + 3]
    out_refs, (x_buf, w_buf, x_sem, w_sem) = refs[blocks + 3 : -4], refs[-4:]
    core = meta_ref[0]
    slice_len, head_cols = wq_ref.shape
    half_cols = head_cols // 2
    cols = w_buf.shape[1] // 3
    heads = cols // HEAD
    for kind in range(3):
        source, first = (wq_ref, 0) if kind == 0 else (wkv_ref, (kind - 1) * head_cols)
        at = pl.multiple_of(first + core * half_cols + group * cols, HEAD)
        own = pl.ds(pl.multiple_of(core * slice_len, 16), slice_len)
        other = pl.ds(pl.multiple_of((1 - core) * slice_len, 16), slice_len)
        there = pl.ds(kind * cols, cols)
        pltpu.make_async_copy(source.at[:, pl.ds(at, cols)], w_buf.at[own, there], w_sem.at[2 * kind]).start()
        pltpu.make_async_copy(
            taken_ref.at[:, pl.ds(kind * half_cols + group * cols, cols)], w_buf.at[other, there], w_sem.at[2 * kind + 1]
        ).start()
    pairs = sorted(range(0, blocks, 2), key=lambda e: -sum(bool(e >> order[0] & 1) for order in orders))
    for e in pairs:
        for c in range(2):
            gather_block(meta_ref[1 + e + c], x_refs, x_buf.at[e + c], x_sem.at[e + c])
    for at in range(6):
        half = pl.ds(0, slice_len)
        pltpu.make_async_copy(
            taken_ref.at[:, pl.ds(0, cols)], w_buf.at[half, pl.ds(0, cols)], w_sem.at[at]
        ).wait()
    group_len = x_buf.shape[1]
    for e in pairs:
        for c in range(2):
            pltpu.make_async_copy(x_refs[0], x_buf.at[e + c], x_sem.at[e + c]).wait()
        tokens = x_buf[e : e + 2].reshape(2 * group_len, x_buf.shape[2])
        product = jnp.dot(tokens, w_buf[...], preferred_element_type=F32).astype(BF16)
        first = 0
        for p, order in enumerate(orders):
            keep_ref, send_ref = out_refs[2 * p], out_refs[2 * p + 1]
            count = keep_ref.shape[2] // (3 * HEAD)
            ranked = slots_in(blocks, order)
            for c in range(2):
                place = ranked.index(e + c)
                ref = keep_ref if place < blocks // 2 else send_ref
                for h in range(count):
                    for kind in range(3):
                        at = kind * cols + (first + h) * HEAD
                        ref[place % (blocks // 2), :, pl.ds((3 * h + kind) * HEAD, HEAD)] = product[
                            c * group_len : (c + 1) * group_len, at : at + HEAD
                        ]
            first += count


def slots_in(blocks, order):
    return sorted(range(blocks), key=lambda e: [e >> bit & 1 for bit in order] + [e & 1])


def project(meta, x_blocks, w_query, w_keyval, taken, group, per_group, orders, counts):
    blocks = len(x_blocks)
    group_len, depth = x_blocks[0].shape
    hbm = pl.BlockSpec(memory_space=pltpu.HBM)
    out_shape = []
    for count in counts:
        out_shape += [jax.ShapeDtypeStruct((blocks // 2, group_len, count * 3 * HEAD), BF16)] * 2
    cols = per_group * 3 * HEAD
    return pl.pallas_call(
        functools.partial(project_kernel, blocks=blocks, group=group, orders=orders),
        out_shape=out_shape,
        in_specs=[pl.BlockSpec(memory_space=pltpu.SMEM)] + [hbm] * (blocks + 3),
        out_specs=[pl.BlockSpec(memory_space=pltpu.VMEM)] * len(out_shape),
        scratch_shapes=[
            pltpu.VMEM((blocks, group_len, depth), BF16),
            pltpu.VMEM((depth, cols), BF16),
            pltpu.SemaphoreType.DMA((blocks,)),
            pltpu.SemaphoreType.DMA((6,)),
        ],
        compiler_params=pltpu.CompilerParams(vmem_limit_bytes=48 * 1024 * 1024),
        cost_estimate=pl.CostEstimate(
            flops=2 * blocks * group_len * depth * cols,
            bytes_accessed=2 * (blocks * group_len * (depth + cols) + depth * cols),
            transcendentals=0,
        ),
    )(meta, *x_blocks, w_query, w_keyval, taken)


def attend_kernel(meta_ref, qkv_ref, k_ref, v_ref, o_ref, nk_ref, nv_ref, *, key_len):
    length = meta_ref[0]
    qkv = qkv_ref[0]
    q, new_k, new_v = qkv[:, :HEAD], qkv[:, HEAD : 2 * HEAD], qkv[:, 2 * HEAD :]
    nk_ref[...] = new_k
    nv_ref[...] = new_v
    group = q.shape[0]
    cache_len = k_ref.shape[1]

    def scores_of(at):
        keys = k_ref[0, at : at + key_len, :]
        scores = lax.dot_general(q, keys, (((1,), (1,)), ((), ())), preferred_element_type=F32)
        positions = at + lax.broadcasted_iota(jnp.int32, (1, key_len), 1)
        return jnp.where(positions < length, scores, -1e30)

    def lane_sum(probs):
        total = probs[:, :HEAD]
        for at in range(HEAD, probs.shape[1], HEAD):
            total = total + probs[:, at : at + HEAD]
        return total

    rows = lax.broadcasted_iota(jnp.int32, (group, group), 0)
    cols = lax.broadcasted_iota(jnp.int32, (group, group), 1)
    scores = lax.dot_general(q, new_k, (((1,), (1,)), ((), ())), preferred_element_type=F32)
    scores = jnp.where(cols <= rows, scores, -1e30)
    following = scores_of(0)
    row_max = jnp.max(scores, axis=1, keepdims=True)
    probs = jnp.exp(scores - row_max)
    row_sum = lane_sum(probs)
    weighted = jnp.dot(probs.astype(BF16), new_v, preferred_element_type=F32)
    for at in range(0, cache_len, key_len):
        scores = following
        if at + key_len < cache_len:
            following = scores_of(at + key_len)
        new_max = jnp.maximum(row_max, jnp.max(scores, axis=1, keepdims=True))
        factor = jnp.exp(row_max - new_max)
        probs = jnp.exp(scores - new_max)
        row_max = new_max
        row_sum = row_sum * factor + lane_sum(probs)
        values = v_ref[0, at : at + key_len, :]
        weighted = weighted * factor + jnp.dot(probs.astype(BF16), values, preferred_element_type=F32)
    total = jnp.sum(row_sum, axis=1, keepdims=True)
    o_ref[...] = (weighted / total).astype(BF16)


def attend(meta, qkv, cache_k, cache_v, base, half):
    heads, group, _ = qkv.shape
    count = heads // 2
    cache_len = cache_k.shape[1]
    key_len = min(512, cache_len)

    def side(i, meta):
        return (i // count) ^ meta[1]

    cached = pl.BlockSpec((1, cache_len, HEAD), lambda i, meta: (0, 0, side(i, meta) * half + base + i % count))
    placed = pl.BlockSpec((group, HEAD), lambda i, meta: (0, side(i, meta) * count + i % count))
    return pl.pallas_call(
        functools.partial(attend_kernel, key_len=key_len),
        out_shape=[jax.ShapeDtypeStruct((group, heads * HEAD), BF16)] * 3,
        grid_spec=pltpu.PrefetchScalarGridSpec(
            num_scalar_prefetch=1,
            grid=(heads,),
            in_specs=[pl.BlockSpec((1, group, 3 * HEAD), lambda i, meta: (i, 0, 0)), cached, cached],
            out_specs=[placed] * 3,
        ),
        compiler_params=pltpu.CompilerParams(vmem_limit_bytes=56 * 1024 * 1024),
        cost_estimate=pl.CostEstimate(
            flops=8 * group * (cache_len + group) * HEAD * heads,
            bytes_accessed=4 * (cache_len + 2 * group) * heads * HEAD,
            transcendentals=group * (cache_len + group) * heads,
        ),
    )(meta, qkv, cache_k, cache_v)


def output_kernel(meta_ref, *refs, blocks, groups, first):
    a_refs = [refs[g * blocks : (g + 1) * blocks] for g in range(groups)]
    w_ref = refs[groups * blocks]
    out_refs, (buf, sem) = refs[groups * blocks + 1 : -2], refs[-2:]
    _, chunk, head_cols = buf.shape
    half = head_cols // 2
    cols = half // groups
    ranked = output_order(blocks)
    for at, e in enumerate(ranked):
        for i in range(blocks):

            @pl.when(meta_ref[e] == i)
            def _(at=at, i=i):
                for g in range(groups):
                    for side in range(2):
                        pltpu.make_async_copy(
                            a_refs[g][i].at[pl.ds(first, chunk), pl.ds(side * cols, cols)],
                            buf.at[at, :, pl.ds(side * half + g * cols, cols)],
                            sem.at[at],
                        ).start()

    quarter = blocks // 4
    for part in range(4):
        for at in range(part * quarter, (part + 1) * quarter):
            pltpu.make_async_copy(buf.at[at], buf.at[at], sem.at[at]).wait()
        tokens = buf[part * quarter : (part + 1) * quarter].reshape(quarter * chunk, head_cols)
        product = jnp.dot(tokens, w_ref[...], preferred_element_type=F32).astype(BF16)
        out_refs[part][...] = product.reshape(out_refs[part].shape)


def output_order(blocks):
    bits = blocks.bit_length() - 1
    return sorted(range(blocks), key=lambda e: [1 - (e & 1), e >> 1 & 1] + [e >> bit & 1 for bit in range(2, bits)])


def output(meta, gathered, w_out, first, chunk):
    groups, blocks = len(gathered), len(gathered[0])
    head_cols, out_cols = w_out.shape
    hbm = pl.BlockSpec(memory_space=pltpu.HBM)
    vmem = pl.BlockSpec(memory_space=pltpu.VMEM)
    return pl.pallas_call(
        functools.partial(output_kernel, blocks=blocks, groups=groups, first=first),
        out_shape=[jax.ShapeDtypeStruct((blocks // 4, chunk, out_cols), BF16)] * 4,
        in_specs=[pl.BlockSpec(memory_space=pltpu.SMEM)] + [hbm] * (groups * blocks) + [vmem],
        out_specs=[vmem] * 4,
        scratch_shapes=[pltpu.VMEM((blocks, chunk, head_cols), BF16), pltpu.SemaphoreType.DMA((blocks,))],
        compiler_params=pltpu.CompilerParams(vmem_limit_bytes=40 * 1024 * 1024),
        cost_estimate=pl.CostEstimate(
            flops=2 * blocks * chunk * head_cols * out_cols,
            bytes_accessed=2 * (blocks * chunk * (head_cols + out_cols) + head_cols * out_cols),
            transcendentals=0,
        ),
    )(meta, *[a for part in gathered for a in part], w_out)


def local(
    rows_n,
    cols_n,
    hidden_in,
    norm_gain,
    norm_bias,
    w_query,
    w_keyval,
    bias_query,
    bias_keyval,
    cache_keys,
    cache_values,
    cache_lengths,
    owner_slot,
    w_out,
    bias_out,
):
    row = lax.axis_index("row")
    col = lax.axis_index("col")
    core = row & 1
    group_len, width = hidden_in.shape
    slice_len, head_cols = w_query.shape
    half = head_cols // HEAD // 2
    half_cols = head_cols // 2
    pairs = rows_n // 2
    row_bits = rows_n.bit_length() - 1
    col_bits = cols_n.bit_length() - 1
    q_scale = HEAD ** (-0.5)
    slot_ids = jnp.arange(rows_n, dtype=jnp.int32)
    is_owner = owner_slot[:, None] == slot_ids[None, :]
    inverse = jnp.sum(jnp.where(is_owner, slot_ids[:, None], 0), axis=0).astype(jnp.int32)

    inputs = hidden_in.astype(F32)
    normed = normalize(inputs, norm_gain, norm_bias).astype(BF16)

    pair_len = 2 * slice_len
    pair = row // 2
    pieces = [lax.dynamic_slice_in_dim(normed, (pair ^ offset) * pair_len, pair_len, 1) for offset in range(pairs)]
    *pieces, w_query, w_keyval = lax.optimization_barrier((*pieces, w_query, w_keyval))
    x_blocks = [None] * rows_n
    for offset in reversed(range(pairs)):
        piece = swap(pieces[offset], "row", 2 * offset, rows_n) if offset else pieces[0]
        x_blocks[2 * offset] = piece
        x_blocks[2 * offset + 1] = swap(piece, "row", 1, rows_n)

    w_flat = w_keyval.reshape(slice_len, 2 * head_cols)
    given = jnp.concatenate(
        [
            lax.dynamic_slice_in_dim(source, first + (1 - core) * half_cols, half_cols, 1)
            for source, first in ((w_query, 0), (w_flat, 0), (w_flat, head_cols))
        ],
        axis=1,
    )
    taken = swap(given, "row", 1, rows_n)

    bias = jnp.concatenate([bias_query[None], bias_keyval], axis=0).reshape(3, 2, half, HEAD).transpose(1, 2, 0, 3)
    bias = lax.dynamic_index_in_dim(bias, core, 0, keepdims=False).reshape(half, 3 * HEAD)
    scale = jnp.concatenate([jnp.full((HEAD,), q_scale, F32), jnp.ones((2 * HEAD,), F32)])

    groups = 3 if half % 3 == 0 else 1
    per_group = half // groups
    counts = [per_group // 2, per_group - per_group // 2] if per_group > 1 else [1]
    pair_bits = list(range(1, row_bits))
    orders = [pair_bits[at % len(pair_bits) :] + pair_bits[: at % len(pair_bits)] for at in range(len(counts))]
    project_meta = jnp.concatenate([core[None], inverse[row ^ slot_ids] ^ row]).astype(jnp.int32)
    attend_meta = jnp.stack([cache_lengths[inverse[row]], core]).astype(jnp.int32)

    projected = [
        project(project_meta, x_blocks, w_query, w_flat, taken, g, per_group, orders, counts) for g in range(groups)
    ]
    key_parts, value_parts, gathered = [], [], []
    for g in range(groups):
        base = g * per_group
        own, other = [], []
        for p, order in enumerate(orders):
            keep, send = projected[g][2 * p : 2 * p + 2]
            terms = [keep]
            for bit in order:
                came = swap(send, "row", 1 << bit, rows_n)
                terms = [t[: came.shape[0]] for t in terms] + [came]
                left = came.shape[0] // 2
                if left > 1:
                    send = sum(t[left:].astype(F32) for t in terms).astype(BF16)
            at = base + sum(counts[:p])
            b = bias[at : at + counts[p]].reshape(-1)
            s = jnp.tile(scale, counts[p])
            mine, theirs = (((sum(t[e].astype(F32) for t in terms) + b) * s).astype(BF16) for e in (0, 1))
            came = swap(theirs, "row", 1, rows_n)
            own += [mine[:, 3 * HEAD * h : 3 * HEAD * (h + 1)] for h in range(counts[p])]
            other += [came[:, 3 * HEAD * h : 3 * HEAD * (h + 1)] for h in range(counts[p])]
        attended, new_k, new_v = attend(attend_meta, jnp.stack(own + other), cache_keys, cache_values, base, half)
        key_parts.append(new_k)
        value_parts.append(new_v)
        every = [None] * rows_n
        for offset in reversed(range(pairs)):
            piece = swap(attended, "row", 2 * offset, rows_n) if offset else attended
            every[2 * offset] = piece
            every[2 * offset + 1] = swap(piece, "row", 1, rows_n)
        gathered.append(every)

    cols = per_group * HEAD
    new_k, new_v = (
        jnp.concatenate([p[:, side * cols : (side + 1) * cols] for side in range(2) for p in parts], axis=1)[None]
        for parts in (key_parts, value_parts)
    )

    places = (owner_slot[row ^ slot_ids] ^ row).astype(jnp.int32)
    shift = row_bits - col_bits
    low_bits = row & ((1 << shift) - 1)
    out_cols = width // cols_n
    residual = lax.dynamic_slice_in_dim(hidden_in, col * out_cols, out_cols, 1).astype(F32) + bias_out
    chunks = 4
    chunk = group_len // chunks
    results = []
    for c in range(chunks):
        send_a, send_b, keep_a, keep_b = output(places, gathered, w_out, c * chunk, chunk)
        held = {0: [keep_a, keep_b], 1: [swap(send_a, "row", 1, rows_n), swap(send_b, "row", 1, rows_n)]}
        for bit in range(1, row_bits):
            mask = 1 << bit
            after = {}
            for j, parts in held.items():
                keep, send = parts if bit == 1 else (parts[: parts.shape[0] // 2], parts[parts.shape[0] // 2 :])
                after[j], after[j | mask] = keep, swap(send, "row", mask, rows_n)
            held = after
            if bit >= shift:
                cmask = 1 << (bit - shift)
                flip = ((row >> bit) ^ (col >> (bit - shift))) & 1
                after = {}
                for j in sorted(held):
                    if j & mask:
                        continue
                    low, high = held[j], held[j | mask]
                    came = swap(jnp.where(flip == 0, high, low), "col", cmask, cols_n)
                    total = jnp.where(flip == 0, low, high).astype(F32) + came.astype(F32)
                    after[j] = total if bit == row_bits - 1 else total.astype(BF16)
                held = after
        count = 1 << shift
        stacked = jnp.concatenate([held[j] for j in range(count)], axis=0)
        results.append(
            jnp.concatenate(
                [lax.dynamic_index_in_dim(stacked, low_bits ^ j, 0, keepdims=False) for j in range(count)], axis=1
            )
        )
    hidden_out = (jnp.concatenate(results, axis=0) + residual).astype(BF16)
    return hidden_out, new_k, new_v


def solution(mesh):
    placed = (
        P("row", None),
        P(),
        P(),
        P("row", "col"),
        P("row", None, "col"),
        P("col"),
        P(None, "col"),
        P("row", None, "col"),
        P("row", None, "col"),
        P(),
        P(),
        P("col", "row"),
        P("col"),
    )
    return jax.shard_map(
        functools.partial(local, mesh.shape["row"], mesh.shape["col"]),
        mesh=mesh,
        in_specs=placed,
        out_specs=(P("row", "col"), P("row", None, "col"), P("row", None, "col")),
        check_vma=False,
    )
```

time: 738 us -> 395 us (0.54)
  waiting for transfers between devices: 452 us -> 179 us
  matrix products: 137 us -> 0 us
  Pallas kernels: 0 us -> 80.9 us
  starting transfers between devices: 0.68 us -> 73.5 us
  local copies, waits for them, and re-layouts: 80 us -> 25.3 us
  other arithmetic: 49.7 us -> 26.5 us
  between operations: 17.5 us -> 3.88 us
    all_gather x6 -> x0, waiting for transfers between devices: 387 us -> none  [the longest x1 195 us: local(): lax.all_gather(w_keyval, 'row', axis=0, tiled=True)]
    ppermute x0 -> x87, waiting for transfers between devices: none -> 179 us  [swap(): return lax.ppermute(value, axis, [(i, i ^ mask) for i in range(size)])]
    dot_general x21 -> x0, matrix products: 137 us -> none  [the longest x9 44 us: visit_block(): jnp.einsum('qhd,khd->hqk', query_heads, key_block, preferred_element_type...]
    pallas_call x0 -> x10, Pallas kernels: none -> 80.9 us  [the longest x3 33.8 us: project(): pl.pallas_call(functools.partial(project_kernel, blocks=blocks, group=gro...]
    ppermute x0 -> x87, starting transfers between devices: none -> 73.5 us  [swap(): return lax.ppermute(value, axis, [(i, i ^ mask) for i in range(size)])]
    reduce_scatter x1 -> x0, waiting for transfers between devices: 62.7 us -> none  [local(): lax.psum_scatter(partial_value.astype(jnp.bfloat16), 'col', scatter_dimen...]
    unnamed x30 -> x85, local copies, waits for them, and re-layouts: 63 us -> 15.9 us
    reduce_sum x10 -> x1, other arithmetic: 31.8 us -> 0.08 us  [local(): jnp.sum(jnp.where(is_owner, slot_ids[:, None], 0), axis=0).astype(jnp.int32)]
  transfers between devices with their start and end apart: 7 -> 87, of which waited for: 5 -> 35; matrix products, arithmetic and copies ran while one was open for 33% -> 5% of each run, Pallas kernels for 0% -> 17%
where the time goes in v1:
time: 395 us; the launch traced here: 389 us
  waiting for transfers between devices  179 us (45%)
  Pallas kernels  80.9 us (20%)
  starting transfers between devices  73.5 us (19%)
  other arithmetic  26.5 us (7%)
  local copies, waits for them, and re-layouts  25.3 us (6%)
    ppermute x87, waiting for transfers between devices, swap(): return lax.ppermute(value, axis, [(i, i ^ mask) for i in range(size)])  179 us
    ppermute x87, starting transfers between devices, swap(): return lax.ppermute(value, axis, [(i, i ^ mask) for i in range(size)])  73.5 us
    pallas_call x3, Pallas kernels, project(): pl.pallas_call(functools.partial(project_kernel, blocks=blocks, group=gro...  33.8 us
    pallas_call x3, Pallas kernels, attend(): pl.pallas_call(functools.partial(attend_kernel, key_len=key_len), out_sha...  31.5 us
    unnamed x85, local copies, waits for them, and re-layouts  15.9 us
    pallas_call x4, Pallas kernels, output(): pl.pallas_call(functools.partial(output_kernel, blocks=blocks, groups=gro...  15.7 us
  transfers between devices with their start and end apart: 87, of which 35 were waited for; matrix products, arithmetic and copies ran while one was open for 5% of the time, Pallas kernels for 17%

profile of v1, /device:TPU:0, one launch (start us, length us, event | category | flops | bytes accessed | tf_op | source)
XLA Modules:
  0.0 388.7 jit_solution(2695065643027420748)
XLA Ops:
  24.9 19.3 %collective-permute-done.1.refs_2_ = bf16[256,1792]{1,0:T(8,128)(2,1)S(1)} collective-permute-done((bf16[256,1792]{1,0:T(8,128)(2,1)S(1)}, bf16[256,1792]{1,0:T(8,128)(2,1)S(1)}, u32[]{:S(2)}, u32[]{:S(2)}) %collective-permute-start.1) | collective-permute-done | bytes 917536 | tf_op jit(solution)/shard_map/ppermute | solution.py:23
  44.2 21.0 %collective-permute-done.3.refs_4_ = bf16[256,1792]{1,0:T(8,128)(2,1)} collective-permute-done((bf16[256,1792]{1,0:T(8,128)(2,1)S(1)}, bf16[256,1792]{1,0:T(8,128)(2,1)}, u32[]{:S(2)}, u32[]{:S(2)}) %collective-permute-start.3) | collective-permute-done | bytes 917536 | tf_op jit(solution)/shard_map/ppermute | solution.py:23
  71.7 11.2 %shard_map.152 = (bf16[4,256,384]{2,1,0:T(8,128)(2,1)S(1)}, bf16[4,256,384]{2,1,0:T(8,128)(2,1)}, bf16[4,256,384]{2,1,0:T(8,128)(2,1)S(1)}, bf16[4,256,384]{2,1,0:T(8,128)(2,1)S(1)}) custom-call(s32[9]{0:T(128)S(1)} %pad_add_fusion.1.meta_ref, bf16[256,1792]{1,0:T(8,128)(2,1)S(1)} %get-tuple-element.46.refs_0_, bf16[256,1792]{1,0:T(8,128)(2,1)S(1)} %copy-done.13, ...), custom_call_target="tpu_custom_call" | custom-call | flops 5637144576 | bytes 13238272 | tf_op jit(solution)/shard_map/pallas_call | solution.py:96
  83.9 11.3 %shard_map.148 = (bf16[4,256,384]{2,1,0:T(8,128)(2,1)S(1)}, bf16[4,256,384]{2,1,0:T(8,128)(2,1)S(1)}, bf16[4,256,384]{2,1,0:T(8,128)(2,1)S(1)}, bf16[4,256,384]{2,1,0:T(8,128)(2,1)}) custom-call(s32[9]{0:T(128)S(1)} %pad_add_fusion.1.meta_ref, bf16[256,1792]{1,0:T(8,128)(2,1)S(1)} %get-tuple-element.46.refs_0_, bf16[256,1792]{1,0:T(8,128)(2,1)S(1)} %copy-done.13, ...), custom_call_target="tpu_custom_call" | custom-call | flops 5637144576 | bytes 13238272 | tf_op jit(solution)/shard_map/pallas_call | solution.py:96
  99.0 11.2 %shard_map.150 = (bf16[4,256,384]{2,1,0:T(8,128)(2,1)S(1)}, bf16[4,256,384]{2,1,0:T(8,128)(2,1)}, bf16[4,256,384]{2,1,0:T(8,128)(2,1)S(1)}, bf16[4,256,384]{2,1,0:T(8,128)(2,1)S(1)}) custom-call(s32[9]{0:T(128)S(1)} %pad_add_fusion.1.meta_ref, bf16[256,1792]{1,0:T(8,128)(2,1)S(1)} %get-tuple-element.46.refs_0_, bf16[256,1792]{1,0:T(8,128)(2,1)S(1)} %copy-done.13, ...), custom_call_target="tpu_custom_call" | custom-call | flops 5637144576 | bytes 13238272 | tf_op jit(solution)/shard_map/pallas_call | solution.py:96
  122.6 11.2 %collective-permute-done.21 = bf16[4,256,384]{2,1,0:T(8,128)(2,1)} collective-permute-done((bf16[4,256,384]{2,1,0:T(8,128)(2,1)}, bf16[4,256,384]{2,1,0:T(8,128)(2,1)}, u32[]{:S(2)}, u32[]{:S(2)}) %collective-permute-start.21) | collective-permute-done | bytes 786464 | tf_op jit(solution)/shard_map/ppermute | solution.py:23
  138.1 14.0 %collective-permute-done.36 = bf16[4,256,384]{2,1,0:T(8,128)(2,1)S(1)} collective-permute-done((bf16[4,256,384]{2,1,0:T(8,128)(2,1)}, bf16[4,256,384]{2,1,0:T(8,128)(2,1)S(1)}, u32[]{:S(2)}, u32[]{:S(2)}) %collective-permute-start.36) | collective-permute-done | bytes 786464 | tf_op jit(solution)/shard_map/ppermute | solution.py:23
  154.4 6.1 %collective-permute-done.35 = bf16[2,256,384]{2,1,0:T(8,128)(2,1)S(1)} collective-permute-done((bf16[2,256,384]{2,1,0:T(8,128)(2,1)S(1)}, bf16[2,256,384]{2,1,0:T(8,128)(2,1)S(1)}, u32[]{:S(2)}, u32[]{:S(2)}) %collective-permute-start.35) | collective-permute-done | bytes 393248 | tf_op jit(solution)/shard_map/ppermute | solution.py:23
  162.8 6.1 %collective-permute-done.22 = bf16[2,256,384]{2,1,0:T(8,128)(2,1)S(1)} collective-permute-done((bf16[2,256,384]{2,1,0:T(8,128)(2,1)S(1)}, bf16[2,256,384]{2,1,0:T(8,128)(2,1)S(1)}, u32[]{:S(2)}, u32[]{:S(2)}) %collective-permute-start.22) | collective-permute-done | bytes 393248 | tf_op jit(solution)/shard_map/ppermute | solution.py:23
  179.9 10.5 %shard_map.149 = (bf16[256,512]{1,0:T(8,128)(2,1)}, bf16[256,512]{1,0:T(8,128)(2,1)}, bf16[256,512]{1,0:T(8,128)(2,1)}) custom-call(s32[2]{0:T(128)} %pad_add_fusion.meta_ref, bf16[4,256,384]{2,1,0:T(8,128)(2,1)} %get-tuple-element.121.qkv_ref, bf16[1,4096,1536]{2,1,0:T(8,128)(2,1)} %k_ref.5, bf16[1,4096,1536]{2,1,0:T(8,128)(2,1)} %v_ref.5), custom_call_target="tpu_custom_call" | custom-call | flops 4563402752 | bytes 9437184 | tf_op jit(solution)/shard_map/pallas_call | solution.py:172
  194.1 10.5 %shard_map.151 = (bf16[256,512]{1,0:T(8,128)(2,1)}, bf16[256,512]{1,0:T(8,128)(2,1)}, bf16[256,512]{1,0:T(8,128)(2,1)}) custom-call(s32[2]{0:T(128)} %pad_add_fusion.meta_ref, bf16[4,256,384]{2,1,0:T(8,128)(2,1)} %get-tuple-element.122.qkv_ref, bf16[1,4096,1536]{2,1,0:T(8,128)(2,1)} %k_ref.5, bf16[1,4096,1536]{2,1,0:T(8,128)(2,1)} %v_ref.5), custom_call_target="tpu_custom_call" | custom-call | flops 4563402752 | bytes 9437184 | tf_op jit(solution)/shard_map/pallas_call | solution.py:172
  205.9 10.5 %shard_map.153 = (bf16[256,512]{1,0:T(8,128)(2,1)}, bf16[256,512]{1,0:T(8,128)(2,1)}, bf16[256,512]{1,0:T(8,128)(2,1)}) custom-call(s32[2]{0:T(128)} %pad_add_fusion.meta_ref, bf16[4,256,384]{2,1,0:T(8,128)(2,1)} %pad_maximum_fusion.3.qkv_ref, bf16[1,4096,1536]{2,1,0:T(8,128)(2,1)} %k_ref.5, bf16[1,4096,1536]{2,1,0:T(8,128)(2,1)} %v_ref.5), custom_call_target="tpu_custom_call" | custom-call | flops 4563402752 | bytes 9437184 | tf_op jit(solution)/shard_map/pallas_call | solution.py:172
  228.6 6.6 %collective-permute-done.30.refs_12_ = bf16[256,512]{1,0:T(8,128)(2,1)S(1)} collective-permute-done((bf16[256,512]{1,0:T(8,128)(2,1)S(1)}, bf16[256,512]{1,0:T(8,128)(2,1)S(1)}, u32[]{:S(2)}, u32[]{:S(2)}) %collective-permute-start.30) | collective-permute-done | bytes 262176 | tf_op jit(solution)/shard_map/ppermute | solution.py:23
  237.6 8.0 %collective-permute-done.43.refs_20_ = bf16[256,512]{1,0:T(8,128)(2,1)S(1)} collective-permute-done((bf16[256,512]{1,0:T(8,128)(2,1)}, bf16[256,512]{1,0:T(8,128)(2,1)S(1)}, u32[]{:S(2)}, u32[]{:S(2)}) %collective-permute-start.43) | collective-permute-done | bytes 262176 | tf_op jit(solution)/shard_map/ppermute | solution.py:23
  265.1 4.1 %shard_map.154 = (bf16[2,64,896]{2,1,0:T(8,128)(2,1)S(1)}, bf16[2,64,896]{2,1,0:T(8,128)(2,1)S(1)}, bf16[2,64,896]{2,1,0:T(8,128)(2,1)S(1)}, bf16[2,64,896]{2,1,0:T(8,128)(2,1)S(1)}) custom-call(s32[8]{0:T(128)S(1)} %broadcast_xor_fusion.1.meta_ref, bf16[256,512]{1,0:T(8,128)(2,1)S(1)} %copy-done.1, bf16[256,512]{1,0:T(8,128)(2,1)S(1)} %collective-permute-done.14.refs_1_, ...), custom_call_target="tpu_custom_call" | custom-call | flops 1409286144 | bytes 5242880 | tf_op jit(solution)/shard_map/pallas_call | solution.py:230
  270.0 7.4 %collective-permute-done.57 = bf16[2,64,896]{2,1,0:T(8,128)(2,1)S(1)} collective-permute-done((bf16[2,64,896]{2,1,0:T(8,128)(2,1)S(1)}, bf16[2,64,896]{2,1,0:T(8,128)(2,1)S(1)}, u32[]{:S(2)}, u32[]{:S(2)}) %collective-permute-start.57) | collective-permute-done | bytes 229408 | tf_op jit(solution)/shard_map/ppermute | solution.py:23
  277.7 6.4 %collective-permute-done.47 = bf16[2,64,896]{2,1,0:T(8,128)(2,1)S(1)} collective-permute-done((bf16[2,64,896]{2,1,0:T(8,128)(2,1)S(1)}, bf16[2,64,896]{2,1,0:T(8,128)(2,1)S(1)}, u32[]{:S(2)}, u32[]{:S(2)}) %collective-permute-start.47) | collective-permute-done | bytes 229408 | tf_op jit(solution)/shard_map/ppermute | solution.py:23
  285.7 4.7 %collective-permute-done.78 = bf16[2,64,896]{2,1,0:T(8,128)(2,1)S(1)} collective-permute-done((bf16[2,64,896]{2,1,0:T(8,128)(2,1)S(1)}, bf16[2,64,896]{2,1,0:T(8,128)(2,1)S(1)}, u32[]{:S(2)}, u32[]{:S(2)}) %collective-permute-start.78) | collective-permute-done | bytes 229408 | tf_op jit(solution)/shard_map/ppermute | solution.py:23
  292.0 5.7 %collective-permute-done.68 = bf16[2,64,896]{2,1,0:T(8,128)(2,1)S(1)} collective-permute-done((bf16[2,64,896]{2,1,0:T(8,128)(2,1)S(1)}, bf16[2,64,896]{2,1,0:T(8,128)(2,1)S(1)}, u32[]{:S(2)}, u32[]{:S(2)}) %collective-permute-start.68) | collective-permute-done | bytes 229408 | tf_op jit(solution)/shard_map/ppermute | solution.py:23
  299.4 6.7 %collective-permute-done.58 = bf16[2,64,896]{2,1,0:T(8,128)(2,1)S(1)} collective-permute-done((bf16[2,64,896]{2,1,0:T(8,128)(2,1)S(1)}, bf16[2,64,896]{2,1,0:T(8,128)(2,1)S(1)}, u32[]{:S(2)}, u32[]{:S(2)}) %collective-permute-start.58) | collective-permute-done | bytes 229408 | tf_op jit(solution)/shard_map/ppermute | solution.py:23
  307.9 4.3 %collective-permute-done.48 = bf16[2,64,896]{2,1,0:T(8,128)(2,1)S(1)} collective-permute-done((bf16[2,64,896]{2,1,0:T(8,128)(2,1)S(1)}, bf16[2,64,896]{2,1,0:T(8,128)(2,1)S(1)}, u32[]{:S(2)}, u32[]{:S(2)}) %collective-permute-start.48) | collective-permute-done | bytes 229408 | tf_op jit(solution)/shard_map/ppermute | solution.py:23
  312.9 7.6 %collective-permute-done.83 = bf16[2,64,896]{2,1,0:T(8,128)(2,1)S(1)} collective-permute-done((bf16[2,64,896]{2,1,0:T(8,128)(2,1)S(1)}, bf16[2,64,896]{2,1,0:T(8,128)(2,1)S(1)}, u32[]{:S(2)}, u32[]{:S(2)}) %collective-permute-start.83) | collective-permute-done | bytes 229408 | tf_op jit(solution)/shard_map/ppermute | solution.py:23
  322.8 6.2 %collective-permute-done.73 = bf16[2,64,896]{2,1,0:T(8,128)(2,1)S(1)} collective-permute-done((bf16[2,64,896]{2,1,0:T(8,128)(2,1)S(1)}, bf16[2,64,896]{2,1,0:T(8,128)(2,1)S(1)}, u32[]{:S(2)}, u32[]{:S(2)}) %collective-permute-start.73) | collective-permute-done | bytes 229408 | tf_op jit(solution)/shard_map/ppermute | solution.py:23
  373.9 8.2 %collective-permute-done.86 = bf16[1,64,896]{2,1,0:T(8,128)(2,1)S(1)} collective-permute-done((bf16[1,64,896]{2,1,0:T(8,128)(2,1)S(1)}, bf16[1,64,896]{2,1,0:T(8,128)(2,1)S(1)}, u32[]{:S(2)}, u32[]{:S(2)}) %collective-permute-start.86) | collective-permute-done | bytes 114720 | tf_op jit(solution)/shard_map/ppermute | solution.py:23
  (329 shorter events, 166.2 us)
Async XLA Ops:
  20.1 49.3 %collective-permute-start.7 = (bf16[896,2304]{1,0:T(8,128)(2,1)}, bf16[896,2304]{1,0:T(8,128)(2,1)}, u32[]{:S(2)}, u32[]{:S(2)}) collective-permute-start(bf16[896,2304]{1,0:T(8,128)(2,1)} %pad_maximum_fusion), channel_id=1, source_target_pairs={{0,4},{4,0},{8,12},{12,8},{16,20},{20,16},{24,28},{28,24},{1,5},{5... | collective-permute-start | bytes 12386312 | tf_op jit(solution)/shard_map/ppermute | solution.py:23
  20.5 23.7 %collective-permute-start.1 = (bf16[256,1792]{1,0:T(8,128)(2,1)S(1)}, bf16[256,1792]{1,0:T(8,128)(2,1)S(1)}, u32[]{:S(2)}, u32[]{:S(2)}) collective-permute-start(bf16[256,1792]{1,0:T(8,128)(2,1)S(1)} %copy-done.21), channel_id=1, source_target_pairs={{0,8},{4,12},{8,0},{12,4},{16,24},{20,28},{24,16},{28,20},{1,9},{5... | collective-permute-start | bytes 2752520 | tf_op jit(solution)/shard_map/ppermute | solution.py:23
  23.0 42.2 %collective-permute-start.3 = (bf16[256,1792]{1,0:T(8,128)(2,1)S(1)}, bf16[256,1792]{1,0:T(8,128)(2,1)}, u32[]{:S(2)}, u32[]{:S(2)}) collective-permute-start(bf16[256,1792]{1,0:T(8,128)(2,1)S(1)} %copy-done.20), channel_id=1, source_target_pairs={{0,16},{4,20},{8,24},{12,28},{16,0},{20,4},{24,8},{28,12},{1,17},{... | collective-permute-start | bytes 2752520 | tf_op jit(solution)/shard_map/ppermute | solution.py:23
  24.5 40.7 %collective-permute-start.5 = (bf16[256,1792]{1,0:T(8,128)(2,1)S(1)}, bf16[256,1792]{1,0:T(8,128)(2,1)}, u32[]{:S(2)}, u32[]{:S(2)}) collective-permute-start(bf16[256,1792]{1,0:T(8,128)(2,1)S(1)} %copy-done.19), channel_id=1, source_target_pairs={{0,24},{4,28},{8,16},{12,20},{16,8},{20,12},{24,0},{28,4},{1,25},{... | collective-permute-start | bytes 2752520 | tf_op jit(solution)/shard_map/ppermute | solution.py:23
  24.9 42.4 %collective-permute-start = (bf16[256,1792]{1,0:T(8,128)(2,1)S(1)}, bf16[256,1792]{1,0:T(8,128)(2,1)S(1)}, u32[]{:S(2)}, u32[]{:S(2)}) collective-permute-start(bf16[256,1792]{1,0:T(8,128)(2,1)S(1)} %get-tuple-element.46.refs_0_), channel_id=1, source_target_pairs={{0,4},{4,0},{8,12},{12,8},{16,20},{20,16},{24,28},{28,24},{1,5},{5... | collective-permute-start | bytes 2752520 | tf_op jit(solution)/shard_map/ppermute | solution.py:23
  44.2 24.0 %collective-permute-start.2 = (bf16[256,1792]{1,0:T(8,128)(2,1)S(1)}, bf16[256,1792]{1,0:T(8,128)(2,1)}, u32[]{:S(2)}, u32[]{:S(2)}) collective-permute-start(bf16[256,1792]{1,0:T(8,128)(2,1)S(1)} %collective-permute-done.1.refs_2_), channel_id=1, source_target_pairs={{0,4},{4,0},{8,12},{12,8},{16,20},{20,16},{24,28},{28,24},{1,5},{5... | collective-permute-start | bytes 2752520 | tf_op jit(solution)/shard_map/ppermute | solution.py:23
  83.9 35.7 %collective-permute-start.34 = (bf16[4,256,384]{2,1,0:T(8,128)(2,1)}, bf16[4,256,384]{2,1,0:T(8,128)(2,1)}, u32[]{:S(2)}, u32[]{:S(2)}) collective-permute-start(bf16[4,256,384]{2,1,0:T(8,128)(2,1)} %get-tuple-element.63), channel_id=1, source_target_pairs={{0,8},{4,12},{8,0},{12,4},{16,24},{20,28},{24,16},{28,20},{1,9},{5... | collective-permute-start | bytes 2359304 | tf_op jit(solution)/shard_map/ppermute | solution.py:23
  97.0 24.2 %collective-permute-start.10 = (bf16[4,256,384]{2,1,0:T(8,128)(2,1)}, bf16[4,256,384]{2,1,0:T(8,128)(2,1)}, u32[]{:S(2)}, u32[]{:S(2)}) collective-permute-start(bf16[4,256,384]{2,1,0:T(8,128)(2,1)} %get-tuple-element.55), channel_id=1, source_target_pairs={{0,16},{4,20},{8,24},{12,28},{16,0},{20,4},{24,8},{28,12},{1,17},{... | collective-permute-start | bytes 2359304 | tf_op jit(solution)/shard_map/ppermute | solution.py:23
  112.9 20.8 %collective-permute-start.21 = (bf16[4,256,384]{2,1,0:T(8,128)(2,1)}, bf16[4,256,384]{2,1,0:T(8,128)(2,1)}, u32[]{:S(2)}, u32[]{:S(2)}) collective-permute-start(bf16[4,256,384]{2,1,0:T(8,128)(2,1)} %get-tuple-element.58), channel_id=1, source_target_pairs={{0,8},{4,12},{8,0},{12,4},{16,24},{20,28},{24,16},{28,20},{1,9},{5... | collective-permute-start | bytes 2359304 | tf_op jit(solution)/shard_map/ppermute | solution.py:23
  114.5 22.0 %collective-permute-start.23 = (bf16[4,256,384]{2,1,0:T(8,128)(2,1)}, bf16[4,256,384]{2,1,0:T(8,128)(2,1)}, u32[]{:S(2)}, u32[]{:S(2)}) collective-permute-start(bf16[4,256,384]{2,1,0:T(8,128)(2,1)} %copy-done.16), channel_id=1, source_target_pairs={{0,16},{4,20},{8,24},{12,28},{16,0},{20,4},{24,8},{28,12},{1,17},{... | collective-permute-start | bytes 2359304 | tf_op jit(solution)/shard_map/ppermute | solution.py:23
  118.1 34.0 %collective-permute-start.36 = (bf16[4,256,384]{2,1,0:T(8,128)(2,1)}, bf16[4,256,384]{2,1,0:T(8,128)(2,1)S(1)}, u32[]{:S(2)}, u32[]{:S(2)}) collective-permute-start(bf16[4,256,384]{2,1,0:T(8,128)(2,1)} %copy-done.15), channel_id=1, source_target_pairs={{0,16},{4,20},{8,24},{12,28},{16,0},{20,4},{24,8},{28,12},{1,17},{... | collective-permute-start | bytes 2359304 | tf_op jit(solution)/shard_map/ppermute | solution.py:23
  119.6 33.6 %collective-permute-start.8 = (bf16[4,256,384]{2,1,0:T(8,128)(2,1)}, bf16[4,256,384]{2,1,0:T(8,128)(2,1)S(1)}, u32[]{:S(2)}, u32[]{:S(2)}) collective-permute-start(bf16[4,256,384]{2,1,0:T(8,128)(2,1)} %copy-done.14), channel_id=1, source_target_pairs={{0,8},{4,12},{8,0},{12,4},{16,24},{20,28},{24,16},{28,20},{1,9},{5... | collective-permute-start | bytes 2359304 | tf_op jit(solution)/shard_map/ppermute | solution.py:23
  121.2 39.3 %collective-permute-start.35 = (bf16[2,256,384]{2,1,0:T(8,128)(2,1)S(1)}, bf16[2,256,384]{2,1,0:T(8,128)(2,1)S(1)}, u32[]{:S(2)}, u32[]{:S(2)}) collective-permute-start(bf16[2,256,384]{2,1,0:T(8,128)(2,1)S(1)} %add_convert_fusion.1), channel_id=1, source_target_pairs={{0,16},{4,20},{8,24},{12,28},{16,0},{20,4},{24,8},{28,12},{1,17},{... | collective-permute-start | bytes 1179656 | tf_op jit(solution)/shard_map/ppermute | solution.py:23
  133.7 29.1 %collective-permute-start.11 = (bf16[2,256,384]{2,1,0:T(8,128)(2,1)S(1)}, bf16[2,256,384]{2,1,0:T(8,128)(2,1)S(1)}, u32[]{:S(2)}, u32[]{:S(2)}) collective-permute-start(bf16[2,256,384]{2,1,0:T(8,128)(2,1)S(1)} %add_convert_fusion.4), channel_id=1, source_target_pairs={{0,8},{4,12},{8,0},{12,4},{16,24},{20,28},{24,16},{28,20},{1,9},{5... | collective-permute-start | bytes 1179656 | tf_op jit(solution)/shard_map/ppermute | solution.py:23
  136.4 32.5 %collective-permute-start.22 = (bf16[2,256,384]{2,1,0:T(8,128)(2,1)S(1)}, bf16[2,256,384]{2,1,0:T(8,128)(2,1)S(1)}, u32[]{:S(2)}, u32[]{:S(2)}) collective-permute-start(bf16[2,256,384]{2,1,0:T(8,128)(2,1)S(1)} %add_convert_fusion.3), channel_id=1, source_target_pairs={{0,16},{4,20},{8,24},{12,28},{16,0},{20,4},{24,8},{28,12},{1,17},{... | collective-permute-start | bytes 1179656 | tf_op jit(solution)/shard_map/ppermute | solution.py:23
  176.1 28.5 %collective-permute-start.39 = (bf16[256,384]{1,0:T(8,128)(2,1)S(1)}, bf16[256,384]{1,0:T(8,128)(2,1)S(1)}, u32[]{:S(2)}, u32[]{:S(2)}) collective-permute-start(bf16[256,384]{1,0:T(8,128)(2,1)S(1)} %get-tuple-element.119), channel_id=1, source_target_pairs={{0,4},{4,0},{8,12},{12,8},{16,20},{20,16},{24,28},{28,24},{1,5},{5... | collective-permute-start | bytes 589832 | tf_op jit(solution)/shard_map/ppermute | solution.py:23
  178.4 26.5 %collective-permute-start.38 = (bf16[256,384]{1,0:T(8,128)(2,1)S(1)}, bf16[256,384]{1,0:T(8,128)(2,1)S(1)}, u32[]{:S(2)}, u32[]{:S(2)}) collective-permute-start(bf16[256,384]{1,0:T(8,128)(2,1)S(1)} %get-tuple-element.115), channel_id=1, source_target_pairs={{0,4},{4,0},{8,12},{12,8},{16,20},{20,16},{24,28},{28,24},{1,5},{5... | collective-permute-start | bytes 589832 | tf_op jit(solution)/shard_map/ppermute | solution.py:23
  190.4 27.2 %collective-permute-start.14 = (bf16[256,512]{1,0:T(8,128)(2,1)}, bf16[256,512]{1,0:T(8,128)(2,1)S(1)}, u32[]{:S(2)}, u32[]{:S(2)}) collective-permute-start(bf16[256,512]{1,0:T(8,128)(2,1)} %get-tuple-element.56.refs_0_), channel_id=1, source_target_pairs={{0,4},{4,0},{8,12},{12,8},{16,20},{20,16},{24,28},{28,24},{1,5},{5... | collective-permute-start | bytes 786440 | tf_op jit(solution)/shard_map/ppermute | solution.py:23
  190.8 29.5 %collective-permute-start.15 = (bf16[256,512]{1,0:T(8,128)(2,1)}, bf16[256,512]{1,0:T(8,128)(2,1)S(1)}, u32[]{:S(2)}, u32[]{:S(2)}) collective-permute-start(bf16[256,512]{1,0:T(8,128)(2,1)} %get-tuple-element.56.refs_0_), channel_id=1, source_target_pairs={{0,8},{4,12},{8,0},{12,4},{16,24},{20,28},{24,16},{28,20},{1,9},{5... | collective-permute-start | bytes 786440 | tf_op jit(solution)/shard_map/ppermute | solution.py:23
  192.5 29.4 %collective-permute-start.17 = (bf16[256,512]{1,0:T(8,128)(2,1)}, bf16[256,512]{1,0:T(8,128)(2,1)S(1)}, u32[]{:S(2)}, u32[]{:S(2)}) collective-permute-start(bf16[256,512]{1,0:T(8,128)(2,1)} %get-tuple-element.56.refs_0_), channel_id=1, source_target_pairs={{0,16},{4,20},{8,24},{12,28},{16,0},{20,4},{24,8},{28,12},{1,17},{... | collective-permute-start | bytes 786440 | tf_op jit(solution)/shard_map/ppermute | solution.py:23
  254.9 52.9 %collective-permute-start.82 = (bf16[2,64,896]{2,1,0:T(8,128)(2,1)S(1)}, bf16[2,64,896]{2,1,0:T(8,128)(2,1)S(1)}, u32[]{:S(2)}, u32[]{:S(2)}) collective-permute-start(bf16[2,64,896]{2,1,0:T(8,128)(2,1)S(1)} %get-tuple-element.82), channel_id=1, source_target_pairs={{0,4},{4,0},{8,12},{12,8},{16,20},{20,16},{24,28},{28,24},{1,5},{5... | collective-permute-start | bytes 688136 | tf_op jit(solution)/shard_map/ppermute | solution.py:23
  255.3 56.9 %collective-permute-start.81 = (bf16[2,64,896]{2,1,0:T(8,128)(2,1)S(1)}, bf16[2,64,896]{2,1,0:T(8,128)(2,1)S(1)}, u32[]{:S(2)}, u32[]{:S(2)}) collective-permute-start(bf16[2,64,896]{2,1,0:T(8,128)(2,1)S(1)} %get-tuple-element.81), channel_id=1, source_target_pairs={{0,4},{4,0},{8,12},{12,8},{16,20},{20,16},{24,28},{28,24},{1,5},{5... | collective-permute-start | bytes 688136 | tf_op jit(solution)/shard_map/ppermute | solution.py:23
  261.3 51.1 %collective-permute-start.72 = (bf16[2,64,896]{2,1,0:T(8,128)(2,1)S(1)}, bf16[2,64,896]{2,1,0:T(8,128)(2,1)S(1)}, u32[]{:S(2)}, u32[]{:S(2)}) collective-permute-start(bf16[2,64,896]{2,1,0:T(8,128)(2,1)S(1)} %get-tuple-element.78), channel_id=1, source_target_pairs={{0,4},{4,0},{8,12},{12,8},{16,20},{20,16},{24,28},{28,24},{1,5},{5... | collective-permute-start | bytes 688136 | tf_op jit(solution)/shard_map/ppermute | solution.py:23
  269.2 51.3 %collective-permute-start.71 = (bf16[2,64,896]{2,1,0:T(8,128)(2,1)S(1)}, bf16[2,64,896]{2,1,0:T(8,128)(2,1)S(1)}, u32[]{:S(2)}, u32[]{:S(2)}) collective-permute-start(bf16[2,64,896]{2,1,0:T(8,128)(2,1)S(1)} %get-tuple-element.77), channel_id=1, source_target_pairs={{0,4},{4,0},{8,12},{12,8},{16,20},{20,16},{24,28},{28,24},{1,5},{5... | collective-permute-start | bytes 688136 | tf_op jit(solution)/shard_map/ppermute | solution.py:23
  (100 other events, 1196.0 us)

commit v2 on v1

--- a/solution.py
+++ b/solution.py
@@ -12,11 +12,39 @@
 BF16 = jnp.bfloat16
 
 
-def normalize(inputs, gain, bias):
-    row_mean = jnp.mean(inputs, axis=-1, keepdims=True)
-    centered = inputs - row_mean
-    row_var = jnp.mean(centered * centered, axis=-1, keepdims=True)
-    return centered * lax.rsqrt(row_var + 1e-05) * gain + bias
+def normalize_kernel(meta_ref, hidden_ref, gain_ref, bias_ref, *out_refs):
+    *piece_refs, core_ref = out_refs
+    core_ref[0] = meta_ref[1]
+    width = hidden_ref.shape[1]
+    length = piece_refs[0].shape[1]
+    rows = hidden_ref[...].astype(F32)
+    mean = jnp.sum(rows, axis=1, keepdims=True) / width
+    centered = rows - mean
+    var = jnp.sum(centered * centered, axis=1, keepdims=True) / width
+    factor = lax.rsqrt(var + 1e-05)
+    for d, ref in enumerate(piece_refs):
+        part = pl.ds(pl.multiple_of((meta_ref[0] ^ d) * length, HEAD), length)
+        ref[...] = ((hidden_ref[:, part].astype(F32) - mean) * factor * gain_ref[:, part] + bias_ref[:, part]).astype(BF16)
+
+
+def normalize(meta, hidden, gain, bias, pairs):
+    rows, width = hidden.shape
+    step = 32
+    whole = pl.BlockSpec((1, width), lambda i, meta: (0, 0))
+    *pieces, core = pl.pallas_call(
+        normalize_kernel,
+        out_shape=[jax.ShapeDtypeStruct((rows, width // pairs), BF16)] * pairs + [jax.ShapeDtypeStruct((1,), jnp.int32)],
+        grid_spec=pltpu.PrefetchScalarGridSpec(
+            num_scalar_prefetch=1,
+            grid=(rows // step,),
+            in_specs=[pl.BlockSpec((step, width), lambda i, meta: (i, 0)), whole, whole],
+            out_specs=[pl.BlockSpec((step, width // pairs), lambda i, meta: (i, 0))] * pairs
+            + [pl.BlockSpec(memory_space=pltpu.SMEM)],
+        ),
+        compiler_params=pltpu.CompilerParams(vmem_limit_bytes=24 * 1024 * 1024),
+        cost_estimate=pl.CostEstimate(flops=10 * rows * width, bytes_accessed=4 * rows * width, transcendentals=rows),
+    )(meta, hidden, gain[None], bias[None])
+    return pieces, core[0]
 
 
 def swap(value, axis, mask, size):
@@ -40,8 +68,8 @@
     cols = w_buf.shape[1] // 3
     heads = cols // HEAD
     for kind in range(3):
-        source, first = (wq_ref, 0) if kind == 0 else (wkv_ref, (kind - 1) * head_cols)
-        at = pl.multiple_of(first + core * half_cols + group * cols, HEAD)
+        source, first = (wq_ref, core * half_cols) if kind == 0 else (wkv_ref, (kind - 1) * half_cols)
+        at = pl.multiple_of(first + group * cols, HEAD)
         own = pl.ds(pl.multiple_of(core * slice_len, 16), slice_len)
         other = pl.ds(pl.multiple_of((1 - core) * slice_len, 16), slice_len)
         there = pl.ds(kind * cols, cols)
@@ -49,28 +77,28 @@
         pltpu.make_async_copy(
             taken_ref.at[:, pl.ds(kind * half_cols + group * cols, cols)], w_buf.at[other, there], w_sem.at[2 * kind + 1]
         ).start()
-    pairs = sorted(range(0, blocks, 2), key=lambda e: -sum(bool(e >> order[0] & 1) for order in orders))
-    for e in pairs:
-        for c in range(2):
-            gather_block(meta_ref[1 + e + c], x_refs, x_buf.at[e + c], x_sem.at[e + c])
+    sequence = sorted(range(blocks), key=lambda e: -sum(bool(e >> order[0] & 1) for order in orders))
+    for at, e in enumerate(sequence):
+        gather_block(meta_ref[1 + e], x_refs, x_buf.at[at], x_sem.at[at])
     for at in range(6):
         half = pl.ds(0, slice_len)
         pltpu.make_async_copy(
             taken_ref.at[:, pl.ds(0, cols)], w_buf.at[half, pl.ds(0, cols)], w_sem.at[at]
         ).wait()
     group_len = x_buf.shape[1]
-    for e in pairs:
-        for c in range(2):
-            pltpu.make_async_copy(x_refs[0], x_buf.at[e + c], x_sem.at[e + c]).wait()
-        tokens = x_buf[e : e + 2].reshape(2 * group_len, x_buf.shape[2])
+    batch = 4
+    for start in range(0, blocks, batch):
+        for at in range(start, start + batch):
+            pltpu.make_async_copy(x_refs[0], x_buf.at[at], x_sem.at[at]).wait()
+        tokens = x_buf[start : start + batch].reshape(batch * group_len, x_buf.shape[2])
         product = jnp.dot(tokens, w_buf[...], preferred_element_type=F32).astype(BF16)
         first = 0
         for p, order in enumerate(orders):
             keep_ref, send_ref = out_refs[2 * p], out_refs[2 * p + 1]
             count = keep_ref.shape[2] // (3 * HEAD)
             ranked = slots_in(blocks, order)
-            for c in range(2):
-                place = ranked.index(e + c)
+            for c in range(batch):
+                place = ranked.index(sequence[start + c])
                 ref = keep_ref if place < blocks // 2 else send_ref
                 for h in range(count):
                     for kind in range(3):
@@ -113,9 +141,60 @@
     )(meta, *x_blocks, w_query, w_keyval, taken)
 
 
-def attend_kernel(meta_ref, qkv_ref, k_ref, v_ref, o_ref, nk_ref, nv_ref, *, key_len):
+def forward_kernel(*refs, parts, terms, behind):
+    out_refs = refs[parts * terms + behind :]
+    for p in range(parts):
+        mine = refs[p * terms : (p + 1) * terms]
+        out_refs[p][...] = sum(ref[...].astype(F32) for ref in mine).astype(BF16)
+
+
+def forward(terms, behind):
+    left = min(t.shape[0] for t in terms[0]) // 2
+    shapes = [(left, *ts[0].shape[1:]) for ts in terms]
+    specs = [pl.BlockSpec(shape, lambda i: (1, 0, 0)) for shape, ts in zip(shapes, terms) for _ in ts]
+    return pl.pallas_call(
+        functools.partial(forward_kernel, parts=len(terms), terms=len(terms[0]), behind=len(behind)),
+        grid=(1,),
+        out_shape=[jax.ShapeDtypeStruct(shape, BF16) for shape in shapes],
+        in_specs=specs + [pl.BlockSpec(memory_space=pltpu.HBM)] * len(behind),
+        out_specs=[pl.BlockSpec(shape, lambda i: (0, 0, 0)) for shape in shapes],
+        compiler_params=pltpu.CompilerParams(vmem_limit_bytes=24 * 1024 * 1024),
+    )(*[t for ts in terms for t in ts], *behind)
+
+
+def settle_kernel(bias_ref, scale_ref, *refs, parts, terms, behind):
+    mine_ref, theirs_ref = refs[parts * terms + behind :]
+    width = mine_ref.shape[2]
+    head = 0
+    for p in range(parts):
+        for h in range(refs[p * terms].shape[2] // width):
+            cols = pl.ds(h * width, width)
+            for e, ref in enumerate((mine_ref, theirs_ref)):
+                total = sum(t[e, :, cols].astype(F32) for t in refs[p * terms : (p + 1) * terms])
+                ref[head] = ((total + bias_ref[head : head + 1, :]) * scale_ref[...]).astype(BF16)
+            head += 1
+
+
+def settle(terms, bias, scale, behind):
+    heads, width = bias.shape
+    rows = terms[0][0].shape[1]
+    specs = [pl.BlockSpec((2, *t.shape[1:]), lambda i: (0, 0, 0)) for ts in terms for t in ts]
+    whole = pl.BlockSpec((heads, rows, width), lambda i: (0, 0, 0))
+    return pl.pallas_call(
+        functools.partial(settle_kernel, parts=len(terms), terms=len(terms[0]), behind=len(behind)),
+        grid=(1,),
+        out_shape=[jax.ShapeDtypeStruct((heads, rows, width), BF16)] * 2,
+        in_specs=[pl.BlockSpec((heads, width), lambda i: (0, 0)), pl.BlockSpec((1, width), lambda i: (0, 0))]
+        + specs
+        + [pl.BlockSpec(memory_space=pltpu.HBM)] * len(behind),
+        out_specs=[whole, whole],
+        compiler_params=pltpu.CompilerParams(vmem_limit_bytes=24 * 1024 * 1024),
+    )(bias, scale, *[t for ts in terms for t in ts], *behind)
+
+
+def attend_kernel(meta_ref, own_ref, other_ref, k_ref, v_ref, o_ref, nk_ref, nv_ref, *, key_len):
     length = meta_ref[0]
-    qkv = qkv_ref[0]
+    qkv = jnp.where(pl.program_id(0) < pl.num_programs(0) // 2, own_ref[0], other_ref[0])
     q, new_k, new_v = qkv[:, :HEAD], qkv[:, HEAD : 2 * HEAD], qkv[:, 2 * HEAD :]
     nk_ref[...] = new_k
     nv_ref[...] = new_v
@@ -158,9 +237,9 @@
     o_ref[...] = (weighted / total).astype(BF16)
 
 
-def attend(meta, qkv, cache_k, cache_v, base, half):
-    heads, group, _ = qkv.shape
-    count = heads // 2
+def attend(meta, own, other, cache_k, cache_v, base, half):
+    count, group, width = own.shape
+    heads = 2 * count
     cache_len = cache_k.shape[1]
     key_len = min(512, cache_len)
 
@@ -175,7 +254,12 @@
         grid_spec=pltpu.PrefetchScalarGridSpec(
             num_scalar_prefetch=1,
             grid=(heads,),
-            in_specs=[pl.BlockSpec((1, group, 3 * HEAD), lambda i, meta: (i, 0, 0)), cached, cached],
+            in_specs=[
+                pl.BlockSpec((1, group, width), lambda i, meta: (jnp.minimum(i, count - 1), 0, 0)),
+                pl.BlockSpec((1, group, width), lambda i, meta: (jnp.maximum(i - count, 0), 0, 0)),
+                cached,
+                cached,
+            ],
             out_specs=[placed] * 3,
         ),
         compiler_params=pltpu.CompilerParams(vmem_limit_bytes=56 * 1024 * 1024),
@@ -184,7 +268,7 @@
             bytes_accessed=4 * (cache_len + 2 * group) * heads * HEAD,
             transcendentals=group * (cache_len + group) * heads,
         ),
-    )(meta, qkv, cache_k, cache_v)
+    )(meta, own, other, cache_k, cache_v)
 
 
 def output_kernel(meta_ref, *refs, blocks, groups, first):
@@ -208,18 +292,18 @@
                             sem.at[at],
                         ).start()
 
-    quarter = blocks // 4
-    for part in range(4):
-        for at in range(part * quarter, (part + 1) * quarter):
+    side = blocks // 2
+    for part in range(2):
+        for at in range(part * side, (part + 1) * side):
             pltpu.make_async_copy(buf.at[at], buf.at[at], sem.at[at]).wait()
-        tokens = buf[part * quarter : (part + 1) * quarter].reshape(quarter * chunk, head_cols)
+        tokens = buf[part * side : (part + 1) * side].reshape(side * chunk, head_cols)
         product = jnp.dot(tokens, w_ref[...], preferred_element_type=F32).astype(BF16)
         out_refs[part][...] = product.reshape(out_refs[part].shape)
 
 
 def output_order(blocks):
     bits = blocks.bit_length() - 1
-    return sorted(range(blocks), key=lambda e: [1 - (e & 1), e >> 1 & 1] + [e >> bit & 1 for bit in range(2, bits)])
+    return sorted(range(blocks), key=lambda e: [1 - (e & 1)] + [e >> bit & 1 for bit in range(1, bits)])
 
 
 def output(meta, gathered, w_out, first, chunk):
@@ -229,9 +313,9 @@
     vmem = pl.BlockSpec(memory_space=pltpu.VMEM)
     return pl.pallas_call(
         functools.partial(output_kernel, blocks=blocks, groups=groups, first=first),
-        out_shape=[jax.ShapeDtypeStruct((blocks // 4, chunk, out_cols), BF16)] * 4,
+        out_shape=[jax.ShapeDtypeStruct((blocks // 2, chunk, out_cols), BF16)] * 2,
         in_specs=[pl.BlockSpec(memory_space=pltpu.SMEM)] + [hbm] * (groups * blocks) + [vmem],
-        out_specs=[vmem] * 4,
+        out_specs=[vmem] * 2,
         scratch_shapes=[pltpu.VMEM((blocks, chunk, head_cols), BF16), pltpu.SemaphoreType.DMA((blocks,))],
         compiler_params=pltpu.CompilerParams(vmem_limit_bytes=40 * 1024 * 1024),
         cost_estimate=pl.CostEstimate(
@@ -274,27 +358,20 @@
     is_owner = owner_slot[:, None] == slot_ids[None, :]
     inverse = jnp.sum(jnp.where(is_owner, slot_ids[:, None], 0), axis=0).astype(jnp.int32)
 
-    inputs = hidden_in.astype(F32)
-    normed = normalize(inputs, norm_gain, norm_bias).astype(BF16)
-
-    pair_len = 2 * slice_len
     pair = row // 2
-    pieces = [lax.dynamic_slice_in_dim(normed, (pair ^ offset) * pair_len, pair_len, 1) for offset in range(pairs)]
-    *pieces, w_query, w_keyval = lax.optimization_barrier((*pieces, w_query, w_keyval))
+    pieces, core_after = normalize(jnp.stack([pair, core]).astype(jnp.int32), hidden_in, norm_gain, norm_bias, pairs)
     x_blocks = [None] * rows_n
     for offset in reversed(range(pairs)):
         piece = swap(pieces[offset], "row", 2 * offset, rows_n) if offset else pieces[0]
         x_blocks[2 * offset] = piece
         x_blocks[2 * offset + 1] = swap(piece, "row", 1, rows_n)
 
-    w_flat = w_keyval.reshape(slice_len, 2 * head_cols)
-    given = jnp.concatenate(
-        [
-            lax.dynamic_slice_in_dim(source, first + (1 - core) * half_cols, half_cols, 1)
-            for source, first in ((w_query, 0), (w_flat, 0), (w_flat, head_cols))
-        ],
-        axis=1,
-    )
+    def half_of(weight, which):
+        part = lax.dynamic_slice_in_dim(weight, which * half_cols, half_cols, weight.ndim - 1)
+        return part.reshape(slice_len, -1)
+
+    w_kept = half_of(w_keyval, core_after)
+    given = jnp.concatenate([half_of(w_query, 1 - core_after), half_of(w_keyval, 1 - core_after)], axis=1)
     taken = swap(given, "row", 1, rows_n)
 
     bias = jnp.concatenate([bias_query[None], bias_keyval], axis=0).reshape(3, 2, half, HEAD).transpose(1, 2, 0, 3)
@@ -310,29 +387,22 @@
     attend_meta = jnp.stack([cache_lengths[inverse[row]], core]).astype(jnp.int32)
 
     projected = [
-        project(project_meta, x_blocks, w_query, w_flat, taken, g, per_group, orders, counts) for g in range(groups)
+        project(project_meta, x_blocks, w_query, w_kept, taken, g, per_group, orders, counts) for g in range(groups)
     ]
-    key_parts, value_parts, gathered = [], [], []
+    key_parts, value_parts, gathered, finished = [], [], [], []
     for g in range(groups):
         base = g * per_group
-        own, other = [], []
-        for p, order in enumerate(orders):
-            keep, send = projected[g][2 * p : 2 * p + 2]
-            terms = [keep]
-            for bit in order:
-                came = swap(send, "row", 1 << bit, rows_n)
-                terms = [t[: came.shape[0]] for t in terms] + [came]
-                left = came.shape[0] // 2
-                if left > 1:
-                    send = sum(t[left:].astype(F32) for t in terms).astype(BF16)
-            at = base + sum(counts[:p])
-            b = bias[at : at + counts[p]].reshape(-1)
-            s = jnp.tile(scale, counts[p])
-            mine, theirs = (((sum(t[e].astype(F32) for t in terms) + b) * s).astype(BF16) for e in (0, 1))
-            came = swap(theirs, "row", 1, rows_n)
-            own += [mine[:, 3 * HEAD * h : 3 * HEAD * (h + 1)] for h in range(counts[p])]
-            other += [came[:, 3 * HEAD * h : 3 * HEAD * (h + 1)] for h in range(counts[p])]
-        attended, new_k, new_v = attend(attend_meta, jnp.stack(own + other), cache_keys, cache_values, base, half)
+        terms = [[projected[g][2 * p]] for p in range(len(orders))]
+        sends = [projected[g][2 * p + 1] for p in range(len(orders))]
+        for at in range(len(pair_bits)):
+            for p, order in enumerate(orders):
+                terms[p].append(swap(sends[p], "row", 1 << order[at], rows_n))
+            if at + 1 < len(pair_bits):
+                sends = forward(terms, finished[: g - 1] if g > 1 else [])
+        mine, theirs = settle(terms, bias[base : base + per_group], scale[None], finished[-1:])
+        came = swap(theirs, "row", 1, rows_n)
+        attended, new_k, new_v = attend(attend_meta, mine, came, cache_keys, cache_values, base, half)
+        finished.append(attended)
         key_parts.append(new_k)
         value_parts.append(new_v)
         every = [None] * rows_n
@@ -357,32 +427,25 @@
     chunk = group_len // chunks
     results = []
     for c in range(chunks):
-        send_a, send_b, keep_a, keep_b = output(places, gathered, w_out, c * chunk, chunk)
-        held = {0: [keep_a, keep_b], 1: [swap(send_a, "row", 1, rows_n), swap(send_b, "row", 1, rows_n)]}
+        send, keep = output(places, gathered, w_out, c * chunk, chunk)
+        held = jnp.stack([keep, swap(send, "row", 1, rows_n)])
         for bit in range(1, row_bits):
-            mask = 1 << bit
-            after = {}
-            for j, parts in held.items():
-                keep, send = parts if bit == 1 else (parts[: parts.shape[0] // 2], parts[parts.shape[0] // 2 :])
-                after[j], after[j | mask] = keep, swap(send, "row", mask, rows_n)
-            held = after
+            count = held.shape[1] // 2
+            keep, came = held[:, :count], swap(held[:, count:], "row", 1 << bit, rows_n)
             if bit >= shift:
-                cmask = 1 << (bit - shift)
                 flip = ((row >> bit) ^ (col >> (bit - shift))) & 1
-                after = {}
-                for j in sorted(held):
-                    if j & mask:
-                        continue
-                    low, high = held[j], held[j | mask]
-                    came = swap(jnp.where(flip == 0, high, low), "col", cmask, cols_n)
-                    total = jnp.where(flip == 0, low, high).astype(F32) + came.astype(F32)
-                    after[j] = total if bit == row_bits - 1 else total.astype(BF16)
-                held = after
+                came, keep = (
+                    swap(jnp.where(flip == 0, came, keep), "col", 1 << (bit - shift), cols_n),
+                    jnp.where(flip == 0, keep, came),
+                )
+                held = keep.astype(F32) + came.astype(F32)
+                held = held if bit == row_bits - 1 else held.astype(BF16)
+            else:
+                held = jnp.concatenate([keep, came], axis=0)
         count = 1 << shift
-        stacked = jnp.concatenate([held[j] for j in range(count)], axis=0)
         results.append(
             jnp.concatenate(
-                [lax.dynamic_index_in_dim(stacked, low_bits ^ j, 0, keepdims=False) for j in range(count)], axis=1
+                [lax.dynamic_index_in_dim(held[:, 0], low_bits ^ j, 0, keepdims=False) for j in range(count)], axis=1
             )
         )
     hidden_out = (jnp.concatenate(results, axis=0) + residual).astype(BF16)

time: 395 us -> 351 us (0.89)
  waiting for transfers between devices: 179 us -> 143 us
  other arithmetic: 26.5 us -> 8.32 us
  starting transfers between devices: 73.5 us -> 58.9 us
  local copies, waits for them, and re-layouts: 25.3 us -> 38.8 us
  Pallas kernels: 80.9 us -> 90.5 us
    ppermute x87 -> x64, waiting for transfers between devices: 179 us -> 143 us  [swap(): return lax.ppermute(value, axis, [(i, i ^ mask) for i in range(size)])]
    ppermute x87 -> x64, starting transfers between devices: 73.5 us -> 58.9 us  [swap(): return lax.ppermute(value, axis, [(i, i ^ mask) for i in range(size)])]
    convert_element_type x19 -> x4, other arithmetic: 13.1 us -> 0.69 us  [local(): held = held if bit == row_bits - 1 else held.astype(BF16)]
    pallas_call x0 -> x7, Pallas kernels: none -> 9.82 us  [the longest x1 5.79 us: normalize(): pl.pallas_call(normalize_kernel, out_shape=[jax.ShapeDtypeStruct((rows, w...]
    unnamed x85 -> x105, local copies, waits for them, and re-layouts: 15.9 us -> 25.4 us
  transfers between devices with their start and end apart: 87 -> 64, of which waited for: 35 -> 19; matrix products, arithmetic and copies ran while one was open for 5% -> 6% of each run, Pallas kernels for 17% -> 20%
where the time goes in v2:
time: 351 us; the launch traced here: 344 us
  waiting for transfers between devices  143 us (41%)
  Pallas kernels  90.5 us (26%)
  starting transfers between devices  58.9 us (17%)
  local copies, waits for them, and re-layouts  38.8 us (11%)
  other arithmetic  8.32 us (2%)
  between operations  4.61 us (1%)
    ppermute x64, waiting for transfers between devices, swap(): return lax.ppermute(value, axis, [(i, i ^ mask) for i in range(size)])  143 us
    ppermute x64, starting transfers between devices, swap(): return lax.ppermute(value, axis, [(i, i ^ mask) for i in range(size)])  58.9 us
    pallas_call x3, Pallas kernels, project(): pl.pallas_call(functools.partial(project_kernel, blocks=blocks, group=gro...  34.6 us
    pallas_call x3, Pallas kernels, attend(): pl.pallas_call(functools.partial(attend_kernel, key_len=key_len), out_sha...  31.9 us
    unnamed x105, local copies, waits for them, and re-layouts  25.4 us
    pallas_call x4, Pallas kernels, output(): pl.pallas_call(functools.partial(output_kernel, blocks=blocks, groups=gro...  14.2 us
  transfers between devices with their start and end apart: 64, of which 19 were waited for; matrix products, arithmetic and copies ran while one was open for 6% of the time, Pallas kernels for 20%

profile of v2, /device:TPU:0, one launch (start us, length us, event | category | flops | bytes accessed | tf_op | source)
XLA Modules:
  0.0 344.5 jit_solution(15866715736893888155)
XLA Ops:
  4.3 5.8 %shard_map.148 = (bf16[256,1792]{1,0:T(8,128)(2,1)S(1)}, bf16[256,1792]{1,0:T(8,128)(2,1)}, bf16[256,1792]{1,0:T(8,128)(2,1)}, bf16[256,1792]{1,0:T(8,128)(2,1)}, s32[1]{0:T(128)}) custom-call(s32[2]{0:T(128)S(1)} %pad_add_fusion.2.meta_ref, bf16[256,7168]{1,0:T(8,128)(2,1)S(1)} %copy-done.3, f32[1,7168]{1,0:T(1,128)S(1)} %bitcast.59, f32[1,7168]{1,0:T(1,128)S(1)} %bitcast.60), custom_call_target="tpu_custom_call" | custom-call | flops 18350080 | bytes 7340032 | tf_op jit(solution)/shard_map/pallas_call | solution.py:34
  11.4 6.4 %constant_dynamic-slice_fusion = (bf16[896,2,768]{2,1,0:T(2,128)(2,1)S(1)}, bf16[896,2,768]{2,1,0:T(2,128)(2,1)S(1)}) fusion(bf16[896,2,1536]{2,1,0:T(2,128)(2,1)} %param.17, s32[]{:T(128)S(6)} %select_n.132, s32[]{:T(128)S(6)} %select_n.131), kind=kLoop, calls=%fused_computation.64 | loop fusion | bytes 11010056 | tf_op jit(solution)/shard_map/dynamic_slice | solution.py:370
  26.4 19.9 %collective-permute-done.1.refs_2_ = bf16[256,1792]{1,0:T(8,128)(2,1)S(1)} collective-permute-done((bf16[256,1792]{1,0:T(8,128)(2,1)}, bf16[256,1792]{1,0:T(8,128)(2,1)S(1)}, u32[]{:S(2)}, u32[]{:S(2)}) %collective-permute-start.1) | collective-permute-done | bytes 917536 | tf_op jit(solution)/shard_map/ppermute | solution.py:51
  46.3 21.0 %collective-permute-done.3.refs_4_ = bf16[256,1792]{1,0:T(8,128)(2,1)} collective-permute-done((bf16[256,1792]{1,0:T(8,128)(2,1)}, bf16[256,1792]{1,0:T(8,128)(2,1)}, u32[]{:S(2)}, u32[]{:S(2)}) %collective-permute-start.3) | collective-permute-done | bytes 917536 | tf_op jit(solution)/shard_map/ppermute | solution.py:51
  72.9 11.5 %shard_map.149 = (bf16[4,256,384]{2,1,0:T(8,128)(2,1)S(1)}, bf16[4,256,384]{2,1,0:T(8,128)(2,1)}, bf16[4,256,384]{2,1,0:T(8,128)(2,1)S(1)}, bf16[4,256,384]{2,1,0:T(8,128)(2,1)}) custom-call(s32[9]{0:T(128)S(1)} %pad_add_fusion.1.meta_ref, bf16[256,1792]{1,0:T(8,128)(2,1)S(1)} %get-tuple-element.49.refs_0_, bf16[256,1792]{1,0:T(8,128)(2,1)S(1)} %copy-done.28, ...), custom_call_target="tpu_custom_call" | custom-call | flops 5637144576 | bytes 13238272 | tf_op jit(solution)/shard_map/pallas_call | solution.py:124
  86.8 17.6 %collective-permute-done.8.refs_1_ = bf16[4,256,384]{2,1,0:T(8,128)(2,1)S(1)} collective-permute-done((bf16[4,256,384]{2,1,0:T(8,128)(2,1)}, bf16[4,256,384]{2,1,0:T(8,128)(2,1)S(1)}, u32[]{:S(2)}, u32[]{:S(2)}) %collective-permute-start.8) | collective-permute-done | bytes 786464 | tf_op jit(solution)/shard_map/ppermute | solution.py:51
  108.4 11.5 %shard_map.153 = (bf16[4,256,384]{2,1,0:T(8,128)(2,1)S(1)}, bf16[4,256,384]{2,1,0:T(8,128)(2,1)}, bf16[4,256,384]{2,1,0:T(8,128)(2,1)S(1)}, bf16[4,256,384]{2,1,0:T(8,128)(2,1)}) custom-call(s32[9]{0:T(128)S(1)} %pad_add_fusion.1.meta_ref, bf16[256,1792]{1,0:T(8,128)(2,1)S(1)} %copy-done.24, bf16[256,1792]{1,0:T(8,128)(2,1)S(1)} %copy-done.29, ...), custom_call_target="tpu_custom_call" | custom-call | flops 5637144576 | bytes 13238272 | tf_op jit(solution)/shard_map/pallas_call | solution.py:124
  125.6 11.5 %shard_map.157 = (bf16[4,256,384]{2,1,0:T(8,128)(2,1)S(1)}, bf16[4,256,384]{2,1,0:T(8,128)(2,1)}, bf16[4,256,384]{2,1,0:T(8,128)(2,1)S(1)}, bf16[4,256,384]{2,1,0:T(8,128)(2,1)}) custom-call(s32[9]{0:T(128)S(1)} %copy-done.31, bf16[256,1792]{1,0:T(8,128)(2,1)S(1)} %copy-done.24, bf16[256,1792]{1,0:T(8,128)(2,1)S(1)} %copy-done.29, ...), custom_call_target="tpu_custom_call" | custom-call | flops 5637144576 | bytes 13238272 | tf_op jit(solution)/shard_map/pallas_call | solution.py:124
  150.6 10.7 %shard_map.152 = (bf16[256,512]{1,0:T(8,128)(2,1)}, bf16[256,512]{1,0:T(8,128)(2,1)}, bf16[256,512]{1,0:T(8,128)(2,1)}) custom-call(s32[2]{0:T(128)} %pad_add_fusion.meta_ref, bf16[2,256,384]{2,1,0:T(8,128)(2,1)} %copy-done.17, bf16[2,256,384]{2,1,0:T(8,128)(2,1)} %collective-permute-done.12.other_ref, bf16[1,4096,1536]{2,1,0:T(8,128)(2,1)} %k_ref.5, ...), custom_call_target="tpu_custom_call" | custom-call | flops 4563402752 | bytes 9437184 | tf_op jit(solution)/shard_map/pallas_call | solution.py:251
  162.8 6.0 %collective-permute-done.22.refs_2_ = bf16[2,256,384]{2,1,0:T(8,128)(2,1)S(1)} collective-permute-done((bf16[2,256,384]{2,1,0:T(8,128)(2,1)S(1)}, bf16[2,256,384]{2,1,0:T(8,128)(2,1)S(1)}, u32[]{:S(2)}, u32[]{:S(2)}) %collective-permute-start.22) | collective-permute-done | bytes 393248 | tf_op jit(solution)/shard_map/ppermute | solution.py:51
  178.3 10.5 %shard_map.156 = (bf16[256,512]{1,0:T(8,128)(2,1)}, bf16[256,512]{1,0:T(8,128)(2,1)}, bf16[256,512]{1,0:T(8,128)(2,1)}) custom-call(s32[2]{0:T(128)} %pad_add_fusion.meta_ref, bf16[2,256,384]{2,1,0:T(8,128)(2,1)} %copy-done.19, bf16[2,256,384]{2,1,0:T(8,128)(2,1)} %copy-done.37, bf16[1,4096,1536]{2,1,0:T(8,128)(2,1)} %k_ref.5, bf16[1,4096,1536]{2,1,0:T(8,128)(2,1)} %v_ref.5), custom_call_target="tpu_custom_call" | custom-call | flops 4563402752 | bytes 9437184 | tf_op jit(solution)/shard_map/pallas_call | solution.py:251
  197.8 10.7 %shard_map.160 = (bf16[256,512]{1,0:T(8,128)(2,1)}, bf16[256,512]{1,0:T(8,128)(2,1)}, bf16[256,512]{1,0:T(8,128)(2,1)}) custom-call(s32[2]{0:T(128)} %pad_add_fusion.meta_ref, bf16[2,256,384]{2,1,0:T(8,128)(2,1)} %copy-done.18, bf16[2,256,384]{2,1,0:T(8,128)(2,1)} %copy-done.36, bf16[1,4096,1536]{2,1,0:T(8,128)(2,1)} %k_ref.5, bf16[1,4096,1536]{2,1,0:T(8,128)(2,1)} %v_ref.5), custom_call_target="tpu_custom_call" | custom-call | flops 4563402752 | bytes 9437184 | tf_op jit(solution)/shard_map/pallas_call | solution.py:251
  220.0 5.3 %collective-permute-done.40.refs_20_ = bf16[256,512]{1,0:T(8,128)(2,1)S(1)} collective-permute-done((bf16[256,512]{1,0:T(8,128)(2,1)}, bf16[256,512]{1,0:T(8,128)(2,1)S(1)}, u32[]{:S(2)}, u32[]{:S(2)}) %collective-permute-start.40) | collective-permute-done | bytes 262176 | tf_op jit(solution)/shard_map/ppermute | solution.py:51
  229.0 3.6 %shard_map.164 = (bf16[4,64,896]{2,1,0:T(8,128)(2,1)S(1)}, bf16[4,64,896]{2,1,0:T(8,128)(2,1)S(1)}) custom-call(s32[8]{0:T(128)S(1)} %broadcast_xor_fusion.1.meta_ref, bf16[256,512]{1,0:T(8,128)(2,1)S(1)} %copy-done.2, bf16[256,512]{1,0:T(8,128)(2,1)S(1)} %collective-permute-done.13.refs_1_, bf16[256,512]{1,0:T(8,128)(2,1)S(1)} %collective-permute-done.14.refs_2_, ...), custom_call_target="tpu_custom_call" | custom-call | flops 1409286144 | bytes 5242880 | tf_op jit(solution)/shard_map/pallas_call | solution.py:314
  240.9 3.6 %shard_map.161 = (bf16[4,64,896]{2,1,0:T(8,128)(2,1)S(1)}, bf16[4,64,896]{2,1,0:T(8,128)(2,1)S(1)}) custom-call(s32[8]{0:T(128)S(1)} %broadcast_xor_fusion.1.meta_ref, bf16[256,512]{1,0:T(8,128)(2,1)S(1)} %copy-done.2, bf16[256,512]{1,0:T(8,128)(2,1)S(1)} %collective-permute-done.13.refs_1_, bf16[256,512]{1,0:T(8,128)(2,1)S(1)} %collective-permute-done.14.refs_2_, ...), custom_call_target="tpu_custom_call" | custom-call | flops 1409286144 | bytes 5242880 | tf_op jit(solution)/shard_map/pallas_call | solution.py:314
  250.3 8.3 %collective-permute-done.60 = bf16[2,2,64,896]{3,2,1,0:T(8,128)(2,1)S(1)} collective-permute-done((bf16[2,2,64,896]{3,2,1,0:T(8,128)(2,1)S(1)}, bf16[2,2,64,896]{3,2,1,0:T(8,128)(2,1)S(1)}, u32[]{:S(2)}, u32[]{:S(2)}) %collective-permute-start.60) | collective-permute-done | bytes 458784 | tf_op jit(solution)/shard_map/ppermute | solution.py:51
  260.3 8.1 %collective-permute-done.55 = bf16[2,2,64,896]{3,2,1,0:T(8,128)(2,1)S(1)} collective-permute-done((bf16[2,2,64,896]{3,2,1,0:T(8,128)(2,1)S(1)}, bf16[2,2,64,896]{3,2,1,0:T(8,128)(2,1)S(1)}, u32[]{:S(2)}, u32[]{:S(2)}) %collective-permute-start.55) | collective-permute-done | bytes 458784 | tf_op jit(solution)/shard_map/ppermute | solution.py:51
  270.1 8.1 %collective-permute-done.50 = bf16[2,2,64,896]{3,2,1,0:T(8,128)(2,1)S(1)} collective-permute-done((bf16[2,2,64,896]{3,2,1,0:T(8,128)(2,1)S(1)}, bf16[2,2,64,896]{3,2,1,0:T(8,128)(2,1)S(1)}, u32[]{:S(2)}, u32[]{:S(2)}) %collective-permute-start.50) | collective-permute-done | bytes 458784 | tf_op jit(solution)/shard_map/ppermute | solution.py:51
  280.0 7.2 %collective-permute-done.45 = bf16[2,2,64,896]{3,2,1,0:T(8,128)(2,1)S(1)} collective-permute-done((bf16[2,2,64,896]{3,2,1,0:T(8,128)(2,1)S(1)}, bf16[2,2,64,896]{3,2,1,0:T(8,128)(2,1)S(1)}, u32[]{:S(2)}, u32[]{:S(2)}) %collective-permute-start.45) | collective-permute-done | bytes 458784 | tf_op jit(solution)/shard_map/ppermute | solution.py:51
  293.4 5.5 %collective-permute-done.46 = bf16[2,2,64,896]{3,2,1,0:T(8,128)(2,1)S(1)} collective-permute-done((bf16[2,2,64,896]{3,2,1,0:T(8,128)(2,1)S(1)}, bf16[2,2,64,896]{3,2,1,0:T(8,128)(2,1)S(1)}, u32[]{:S(2)}, u32[]{:S(2)}) %collective-permute-start.46) | collective-permute-done | bytes 458784 | tf_op jit(solution)/shard_map/ppermute | solution.py:51
  313.0 15.2 %collective-permute-done.63 = bf16[2,1,64,896]{3,2,1,0:T(8,128)(2,1)S(1)} collective-permute-done((bf16[2,1,64,896]{3,2,1,0:T(8,128)(2,1)S(1)}, bf16[2,1,64,896]{3,2,1,0:T(8,128)(2,1)S(1)}, u32[]{:S(2)}, u32[]{:S(2)}) %collective-permute-start.63) | collective-permute-done | bytes 229408 | tf_op jit(solution)/shard_map/ppermute | solution.py:51
  328.4 4.8 %collective-permute-done.58 = bf16[2,1,64,896]{3,2,1,0:T(8,128)(2,1)S(1)} collective-permute-done((bf16[2,1,64,896]{3,2,1,0:T(8,128)(2,1)S(1)}, bf16[2,1,64,896]{3,2,1,0:T(8,128)(2,1)S(1)}, u32[]{:S(2)}, u32[]{:S(2)}) %collective-permute-start.58) | collective-permute-done | bytes 229408 | tf_op jit(solution)/shard_map/ppermute | solution.py:51
  333.2 4.8 %collective-permute-done.53 = bf16[2,1,64,896]{3,2,1,0:T(8,128)(2,1)S(1)} collective-permute-done((bf16[2,1,64,896]{3,2,1,0:T(8,128)(2,1)S(1)}, bf16[2,1,64,896]{3,2,1,0:T(8,128)(2,1)S(1)}, u32[]{:S(2)}, u32[]{:S(2)}) %collective-permute-start.53) | collective-permute-done | bytes 229408 | tf_op jit(solution)/shard_map/ppermute | solution.py:51
  338.2 3.6 %collective-permute-done.48 = bf16[2,1,64,896]{3,2,1,0:T(8,128)(2,1)S(1)} collective-permute-done((bf16[2,1,64,896]{3,2,1,0:T(8,128)(2,1)S(1)}, bf16[2,1,64,896]{3,2,1,0:T(8,128)(2,1)S(1)}, u32[]{:S(2)}, u32[]{:S(2)}) %collective-permute-start.48) | collective-permute-done | bytes 229408 | tf_op jit(solution)/shard_map/ppermute | solution.py:51
  (276 shorter events, 118.5 us)
Async XLA Ops:
  21.9 49.8 %collective-permute-start.7 = (bf16[896,2304]{1,0:T(8,128)(2,1)}, bf16[896,2304]{1,0:T(8,128)(2,1)}, u32[]{:S(2)}, u32[]{:S(2)}) collective-permute-start(bf16[896,2304]{1,0:T(8,128)(2,1)} %pad_maximum_fusion), channel_id=1, source_target_pairs={{0,4},{4,0},{8,12},{12,8},{16,20},{20,16},{24,28},{28,24},{1,5},{5... | collective-permute-start | bytes 12386312 | tf_op jit(solution)/shard_map/ppermute | solution.py:51
  22.4 23.9 %collective-permute-start.1 = (bf16[256,1792]{1,0:T(8,128)(2,1)}, bf16[256,1792]{1,0:T(8,128)(2,1)S(1)}, u32[]{:S(2)}, u32[]{:S(2)}) collective-permute-start(bf16[256,1792]{1,0:T(8,128)(2,1)} %get-tuple-element.50), channel_id=1, source_target_pairs={{0,8},{4,12},{8,0},{12,4},{16,24},{20,28},{24,16},{28,20},{1,9},{5... | collective-permute-start | bytes 2752520 | tf_op jit(solution)/shard_map/ppermute | solution.py:51
  24.8 42.5 %collective-permute-start.3 = (bf16[256,1792]{1,0:T(8,128)(2,1)}, bf16[256,1792]{1,0:T(8,128)(2,1)}, u32[]{:S(2)}, u32[]{:S(2)}) collective-permute-start(bf16[256,1792]{1,0:T(8,128)(2,1)} %get-tuple-element.51), channel_id=1, source_target_pairs={{0,16},{4,20},{8,24},{12,28},{16,0},{20,4},{24,8},{28,12},{1,17},{... | collective-permute-start | bytes 2752520 | tf_op jit(solution)/shard_map/ppermute | solution.py:51
  26.4 40.9 %collective-permute-start.5 = (bf16[256,1792]{1,0:T(8,128)(2,1)}, bf16[256,1792]{1,0:T(8,128)(2,1)}, u32[]{:S(2)}, u32[]{:S(2)}) collective-permute-start(bf16[256,1792]{1,0:T(8,128)(2,1)} %get-tuple-element.52), channel_id=1, source_target_pairs={{0,24},{4,28},{8,16},{12,20},{16,8},{20,12},{24,0},{28,4},{1,25},{... | collective-permute-start | bytes 2752520 | tf_op jit(solution)/shard_map/ppermute | solution.py:51
  26.4 44.4 %collective-permute-start = (bf16[256,1792]{1,0:T(8,128)(2,1)S(1)}, bf16[256,1792]{1,0:T(8,128)(2,1)S(1)}, u32[]{:S(2)}, u32[]{:S(2)}) collective-permute-start(bf16[256,1792]{1,0:T(8,128)(2,1)S(1)} %get-tuple-element.49.refs_0_), channel_id=1, source_target_pairs={{0,4},{4,0},{8,12},{12,8},{16,20},{20,16},{24,28},{28,24},{1,5},{5... | collective-permute-start | bytes 2752520 | tf_op jit(solution)/shard_map/ppermute | solution.py:51
  46.3 25.4 %collective-permute-start.2 = (bf16[256,1792]{1,0:T(8,128)(2,1)S(1)}, bf16[256,1792]{1,0:T(8,128)(2,1)}, u32[]{:S(2)}, u32[]{:S(2)}) collective-permute-start(bf16[256,1792]{1,0:T(8,128)(2,1)S(1)} %collective-permute-done.1.refs_2_), channel_id=1, source_target_pairs={{0,4},{4,0},{8,12},{12,8},{16,20},{20,16},{24,28},{28,24},{1,5},{5... | collective-permute-start | bytes 2752520 | tf_op jit(solution)/shard_map/ppermute | solution.py:51
  84.5 20.0 %collective-permute-start.8 = (bf16[4,256,384]{2,1,0:T(8,128)(2,1)}, bf16[4,256,384]{2,1,0:T(8,128)(2,1)S(1)}, u32[]{:S(2)}, u32[]{:S(2)}) collective-permute-start(bf16[4,256,384]{2,1,0:T(8,128)(2,1)} %get-tuple-element.55), channel_id=1, source_target_pairs={{0,8},{4,12},{8,0},{12,4},{16,24},{20,28},{24,16},{28,20},{1,9},{5... | collective-permute-start | bytes 2359304 | tf_op jit(solution)/shard_map/ppermute | solution.py:51
  85.7 19.9 %collective-permute-start.9 = (bf16[4,256,384]{2,1,0:T(8,128)(2,1)}, bf16[4,256,384]{2,1,0:T(8,128)(2,1)S(1)}, u32[]{:S(2)}, u32[]{:S(2)}) collective-permute-start(bf16[4,256,384]{2,1,0:T(8,128)(2,1)} %get-tuple-element.57), channel_id=1, source_target_pairs={{0,16},{4,20},{8,24},{12,28},{16,0},{20,4},{24,8},{28,12},{1,17},{... | collective-permute-start | bytes 2359304 | tf_op jit(solution)/shard_map/ppermute | solution.py:51
  120.5 28.3 %collective-permute-start.20 = (bf16[4,256,384]{2,1,0:T(8,128)(2,1)}, bf16[4,256,384]{2,1,0:T(8,128)(2,1)S(1)}, u32[]{:S(2)}, u32[]{:S(2)}) collective-permute-start(bf16[4,256,384]{2,1,0:T(8,128)(2,1)} %get-tuple-element.64), channel_id=1, source_target_pairs={{0,8},{4,12},{8,0},{12,4},{16,24},{20,28},{24,16},{28,20},{1,9},{5... | collective-permute-start | bytes 2359304 | tf_op jit(solution)/shard_map/ppermute | solution.py:51
  121.3 27.6 %collective-permute-start.21 = (bf16[4,256,384]{2,1,0:T(8,128)(2,1)}, bf16[4,256,384]{2,1,0:T(8,128)(2,1)S(1)}, u32[]{:S(2)}, u32[]{:S(2)}) collective-permute-start(bf16[4,256,384]{2,1,0:T(8,128)(2,1)} %get-tuple-element.66), channel_id=1, source_target_pairs={{0,16},{4,20},{8,24},{12,28},{16,0},{20,4},{24,8},{28,12},{1,17},{... | collective-permute-start | bytes 2359304 | tf_op jit(solution)/shard_map/ppermute | solution.py:51
  125.6 25.0 %collective-permute-start.12 = (bf16[2,256,384]{2,1,0:T(8,128)(2,1)S(1)}, bf16[2,256,384]{2,1,0:T(8,128)(2,1)}, u32[]{:S(2)}, u32[]{:S(2)}) collective-permute-start(bf16[2,256,384]{2,1,0:T(8,128)(2,1)S(1)} %get-tuple-element.61), channel_id=1, source_target_pairs={{0,4},{4,0},{8,12},{12,8},{16,20},{20,16},{24,28},{28,24},{1,5},{5... | collective-permute-start | bytes 1179656 | tf_op jit(solution)/shard_map/ppermute | solution.py:51
  138.9 34.2 %collective-permute-start.32 = (bf16[4,256,384]{2,1,0:T(8,128)(2,1)}, bf16[4,256,384]{2,1,0:T(8,128)(2,1)}, u32[]{:S(2)}, u32[]{:S(2)}) collective-permute-start(bf16[4,256,384]{2,1,0:T(8,128)(2,1)} %get-tuple-element.73), channel_id=1, source_target_pairs={{0,8},{4,12},{8,0},{12,4},{16,24},{20,28},{24,16},{28,20},{1,9},{5... | collective-permute-start | bytes 2359304 | tf_op jit(solution)/shard_map/ppermute | solution.py:51
  140.5 32.7 %collective-permute-start.33 = (bf16[4,256,384]{2,1,0:T(8,128)(2,1)}, bf16[4,256,384]{2,1,0:T(8,128)(2,1)}, u32[]{:S(2)}, u32[]{:S(2)}) collective-permute-start(bf16[4,256,384]{2,1,0:T(8,128)(2,1)} %get-tuple-element.75), channel_id=1, source_target_pairs={{0,16},{4,20},{8,24},{12,28},{16,0},{20,4},{24,8},{28,12},{1,17},{... | collective-permute-start | bytes 2359304 | tf_op jit(solution)/shard_map/ppermute | solution.py:51
  161.3 27.5 %collective-permute-start.14 = (bf16[256,512]{1,0:T(8,128)(2,1)}, bf16[256,512]{1,0:T(8,128)(2,1)S(1)}, u32[]{:S(2)}, u32[]{:S(2)}) collective-permute-start(bf16[256,512]{1,0:T(8,128)(2,1)} %get-tuple-element.62.refs_6_.refs_4_.refs_0_), channel_id=1, source_target_pairs={{0,8},{4,12},{8,0},{12,4},{16,24},{20,28},{24,16},{28,20},{1,9},{5... | collective-permute-start | bytes 786440 | tf_op jit(solution)/shard_map/ppermute | solution.py:51
  168.8 20.2 %collective-permute-start.16 = (bf16[256,512]{1,0:T(8,128)(2,1)}, bf16[256,512]{1,0:T(8,128)(2,1)S(1)}, u32[]{:S(2)}, u32[]{:S(2)}) collective-permute-start(bf16[256,512]{1,0:T(8,128)(2,1)} %get-tuple-element.62.refs_6_.refs_4_.refs_0_), channel_id=1, source_target_pairs={{0,16},{4,20},{8,24},{12,28},{16,0},{20,4},{24,8},{28,12},{1,17},{... | collective-permute-start | bytes 786440 | tf_op jit(solution)/shard_map/ppermute | solution.py:51
  246.8 21.7 %collective-permute-start.55 = (bf16[2,2,64,896]{3,2,1,0:T(8,128)(2,1)S(1)}, bf16[2,2,64,896]{3,2,1,0:T(8,128)(2,1)S(1)}, u32[]{:S(2)}, u32[]{:S(2)}) collective-permute-start(bf16[2,2,64,896]{3,2,1,0:T(8,128)(2,1)S(1)} %pad_maximum_fusion.2), channel_id=1, source_target_pairs={{0,8},{4,12},{8,0},{12,4},{16,24},{20,28},{24,16},{28,20},{1,9},{5... | collective-permute-start | bytes 1376264 | tf_op jit(solution)/shard_map/ppermute | solution.py:51
  248.1 30.2 %collective-permute-start.50 = (bf16[2,2,64,896]{3,2,1,0:T(8,128)(2,1)S(1)}, bf16[2,2,64,896]{3,2,1,0:T(8,128)(2,1)S(1)}, u32[]{:S(2)}, u32[]{:S(2)}) collective-permute-start(bf16[2,2,64,896]{3,2,1,0:T(8,128)(2,1)S(1)} %pad_maximum_fusion.3), channel_id=1, source_target_pairs={{0,8},{4,12},{8,0},{12,4},{16,24},{20,28},{24,16},{28,20},{1,9},{5... | collective-permute-start | bytes 1376264 | tf_op jit(solution)/shard_map/ppermute | solution.py:51
  249.0 38.1 %collective-permute-start.45 = (bf16[2,2,64,896]{3,2,1,0:T(8,128)(2,1)S(1)}, bf16[2,2,64,896]{3,2,1,0:T(8,128)(2,1)S(1)}, u32[]{:S(2)}, u32[]{:S(2)}) collective-permute-start(bf16[2,2,64,896]{3,2,1,0:T(8,128)(2,1)S(1)} %pad_maximum_fusion.4), channel_id=1, source_target_pairs={{0,8},{4,12},{8,0},{12,4},{16,24},{20,28},{24,16},{28,20},{1,9},{5... | collective-permute-start | bytes 1376264 | tf_op jit(solution)/shard_map/ppermute | solution.py:51
  258.7 30.2 %collective-permute-start.61 = (bf16[2,2,64,896]{3,2,1,0:T(8,128)(2,1)S(1)}, bf16[2,2,64,896]{3,2,1,0:T(8,128)(2,1)S(1)}, u32[]{:S(2)}, u32[]{:S(2)}) collective-permute-start(bf16[2,2,64,896]{3,2,1,0:T(8,128)(2,1)S(1)} %broadcast_select_fusion), channel_id=1, source_target_pairs={{0,1},{1,0},{2,3},{3,2},{4,5},{5,4},{6,7},{7,6},{8,9},{9,8},{10,11... | collective-permute-start | bytes 1376264 | tf_op jit(solution)/shard_map/ppermute | solution.py:51
  268.5 22.4 %collective-permute-start.56 = (bf16[2,2,64,896]{3,2,1,0:T(8,128)(2,1)S(1)}, bf16[2,2,64,896]{3,2,1,0:T(8,128)(2,1)S(1)}, u32[]{:S(2)}, u32[]{:S(2)}) collective-permute-start(bf16[2,2,64,896]{3,2,1,0:T(8,128)(2,1)S(1)} %broadcast_select_fusion.1), channel_id=1, source_target_pairs={{0,1},{1,0},{2,3},{3,2},{4,5},{5,4},{6,7},{7,6},{8,9},{9,8},{10,11... | collective-permute-start | bytes 1376264 | tf_op jit(solution)/shard_map/ppermute | solution.py:51
  300.9 27.3 %collective-permute-start.63 = (bf16[2,1,64,896]{3,2,1,0:T(8,128)(2,1)S(1)}, bf16[2,1,64,896]{3,2,1,0:T(8,128)(2,1)S(1)}, u32[]{:S(2)}, u32[]{:S(2)}) collective-permute-start(bf16[2,1,64,896]{3,2,1,0:T(8,128)(2,1)S(1)} %broadcast_select_fusion.4), channel_id=1, source_target_pairs={{0,2},{1,3},{2,0},{3,1},{4,6},{5,7},{6,4},{7,5},{8,10},{9,11},{10,... | collective-permute-start | bytes 688136 | tf_op jit(solution)/shard_map/ppermute | solution.py:51
  303.6 29.5 %collective-permute-start.58 = (bf16[2,1,64,896]{3,2,1,0:T(8,128)(2,1)S(1)}, bf16[2,1,64,896]{3,2,1,0:T(8,128)(2,1)S(1)}, u32[]{:S(2)}, u32[]{:S(2)}) collective-permute-start(bf16[2,1,64,896]{3,2,1,0:T(8,128)(2,1)S(1)} %broadcast_select_fusion.5), channel_id=1, source_target_pairs={{0,2},{1,3},{2,0},{3,1},{4,6},{5,7},{6,4},{7,5},{8,10},{9,11},{10,... | collective-permute-start | bytes 688136 | tf_op jit(solution)/shard_map/ppermute | solution.py:51
  307.6 30.5 %collective-permute-start.53 = (bf16[2,1,64,896]{3,2,1,0:T(8,128)(2,1)S(1)}, bf16[2,1,64,896]{3,2,1,0:T(8,128)(2,1)S(1)}, u32[]{:S(2)}, u32[]{:S(2)}) collective-permute-start(bf16[2,1,64,896]{3,2,1,0:T(8,128)(2,1)S(1)} %broadcast_select_fusion.6), channel_id=1, source_target_pairs={{0,2},{1,3},{2,0},{3,1},{4,6},{5,7},{6,4},{7,5},{8,10},{9,11},{10,... | collective-permute-start | bytes 688136 | tf_op jit(solution)/shard_map/ppermute | solution.py:51
  310.4 31.4 %collective-permute-start.48 = (bf16[2,1,64,896]{3,2,1,0:T(8,128)(2,1)S(1)}, bf16[2,1,64,896]{3,2,1,0:T(8,128)(2,1)S(1)}, u32[]{:S(2)}, u32[]{:S(2)}) collective-permute-start(bf16[2,1,64,896]{3,2,1,0:T(8,128)(2,1)S(1)} %broadcast_select_fusion.7), channel_id=1, source_target_pairs={{0,2},{1,3},{2,0},{3,1},{4,6},{5,7},{6,4},{7,5},{8,10},{9,11},{10,... | collective-permute-start | bytes 688136 | tf_op jit(solution)/shard_map/ppermute | solution.py:51
  (87 other events, 899.2 us)
